TPU v7x, 256 devices: a whole 4x4x8 slice. The times are simulated.
256 devices in a mesh: sec: 8 (over y, core), blk: 32 (over z, x).
Axes of the slice: x: 4, y: 4, z: 8, core: 2. Of those that a mesh axis runs over, the one named last changes fastest.
Arguments:
- env_left: bfloat16 [26, 32, 128, 128], P(None, 'blk'), may hold values from -6 to 6
- transfer: bfloat16 [8, 32, 3, 128, 128], P('sec', 'blk'), may hold values from -0.375 to 0.375
- mpo_mix: float32 [8, 26, 26], P('sec'), may hold values from -1.25 to 1.25
- right_env: bfloat16 [8, 26, 32, 128, 128], P('sec', None, 'blk'), may hold values from -1 to 1
- start_state: float32 [8, 32, 128, 128], P('sec', 'blk'), may hold values from -0.00015258789 to 0.00015258789
- block_rank: int32 [32], P('blk'), may hold values from 1 to 128, as said below
Outputs:
- state: float32 [8, 32, 128, 128], P('sec', 'blk')
- environment: bfloat16 [8, 26, 32, 128, 128], P('sec', None, 'blk')
Inputs may be any that keep to these rules, and one draw needn't show every extreme that they name: `block_rank`: one block has rank exactly 128.
All inputs are finite; a program needn't handle non-finite values.
Results may differ from a plain program's by a relative error of at most 0.04.
Values may be sent and summed in bfloat16 or wider, within the bound.
A program may use at most 64 MiB of HBM per device.

v0:
```python
import jax
import jax.numpy as jnp
from jax import lax
from jax.sharding import PartitionSpec as P

ITERS = 4


def padded_2(block, sides, width):
    for axis, dim in sides:
        count = lax.axis_size(axis)
        forward = [(i, i + 1) for i in range(count - 1)]
        backward = [(target, source) for source, target in forward]
        low = lax.ppermute(
            lax.slice_in_dim(block, block.shape[dim] - width, None, axis=dim), axis, forward
        )
        high = lax.ppermute(lax.slice_in_dim(block, 0, width, axis=dim), axis, backward)
        block = jnp.concatenate([low, block, high], axis=dim)
    return block


def shifted(value, axis, steps):
    count = lax.axis_size(axis)
    leading, last = (max(0, -steps), min(count, count - steps))
    return lax.ppermute(value, axis, [(source, source + steps) for source in range(leading, last)])


def apply_mix(mix, total):
    mixed = jnp.einsum("vw,wqil->vqil", mix, total, precision=lax.Precision.HIGHEST)
    return mixed.astype(jnp.bfloat16)


def padded_step(padded, trans, mix):
    count = padded.shape[1] - 2
    total = None
    for d in range(3):
        source = padded[:, d : d + count]
        tensor = trans[:, d]
        left = jnp.einsum(
            "qji,wqjk->wqik", tensor, source, preferred_element_type=jnp.float32
        ).astype(jnp.bfloat16)
        term = jnp.einsum("wqik,qkl->wqil", left, tensor, preferred_element_type=jnp.float32)
        total = term if total is None else total + term
    return apply_mix(mix, total)


def pull_step(env, trans, mix):
    padded = padded_2(env, (("blk", 1),), 1)
    return padded_step(padded, trans, mix)


def per_device(env_left, transfer, mpo_mix, right_env, start_state, block_rank):
    trans = transfer[0]
    mix = mpo_mix[0]
    section = lax.axis_index("sec")
    env = env_left
    for round_index in range(lax.axis_size("sec") - 1):
        outgoing = pull_step(env, trans, mix)
        moved = shifted(outgoing, "sec", 1)
        env = jnp.where(section == 0, env_left, moved)
    count = env.shape[1]
    size = env.shape[2]
    entries = count * lax.axis_size("blk") * size * size
    index = jnp.arange(size, dtype=jnp.int32)
    keep = (index[None, :] < block_rank[:, None]).astype(jnp.float32)
    mask = keep[:, :, None] * keep[:, None, :]
    renv = right_env[0]
    psi = start_state[0] * mask
    for step in range(ITERS):
        value = psi.astype(jnp.bfloat16)
        padded = padded_2(psi.astype(jnp.bfloat16), (("blk", 0),), 1).astype(psi.dtype)
        left = jnp.einsum("wqij,qjk->wqik", env, value, preferred_element_type=jnp.float32).astype(
            jnp.bfloat16
        )
        applied = jnp.einsum("wqik,wqkl->qil", left, renv, preferred_element_type=jnp.float32)
        applied = applied + 0.5 * (padded[:-2] + padded[2:])
        psi = applied * mask
        total = lax.psum(jnp.sum(psi * psi), "blk")
        psi = psi / jnp.sqrt(total / entries + 1e-06)
    return (psi[None], env[None])


def solution(mesh):
    in_specs = (
        P(None, "blk", None, None),
        P("sec", "blk", None, None, None),
        P("sec", None, None),
        P("sec", None, "blk", None, None),
        P("sec", "blk", None, None),
        P("blk"),
    )
    out_specs = (P("sec", "blk", None, None), P("sec", None, "blk", None, None))
    return jax.shard_map(
        per_device, mesh=mesh, in_specs=in_specs, out_specs=out_specs, check_vma=False
    )
```

profile of v0, /device:TPU:136, one launch (start us, length us, event | category | flops | bytes accessed | tf_op | source)
XLA Modules:
  0.0 699.3 jit_solution(10523690284359027912)
XLA Ops:
  3.0 3.4 collective-permute-start
  6.4 5.8 collective-permute-start.1
  13.0 16.2 %collective-permute-done = bf16[26,1,128,128]{2,3,0,1:T(8,128)(2,1)} collective-permute-done((bf16[26,1,128,128]{2,3,0,1:T(8,128)(2,1)}, bf16[26,1,128,128]{2,3,0,1:T(8,128)(2,1)}, u32[]{:S(2)}, u32[]{:S(2)}) %collective-permute-start) | collective-permute-done | bytes 852000 | tf_op jit(solution)/shard_map/ppermute | solution.py:14
  35.4 6.9 fusion.27
  44.6 12.1 %collective-permute-done.2 = bf16[26,1,128,128]{3,2,1,0:T(8,128)(2,1)S(1)} collective-permute-done((bf16[26,1,128,128]{3,2,1,0:T(8,128)(2,1)S(1)}, bf16[26,1,128,128]{3,2,1,0:T(8,128)(2,1)S(1)}, u32[]{:S(2)}, u32[]{:S(2)}) %collective-permute-start.2) | collective-permute-done | bytes 852000 | tf_op jit(solution)/shard_map/ppermute | solution.py:25
  59.5 7.8 %collective-permute-start.4 = (bf16[26,1,128,128]{3,2,1,0:T(8,128)(2,1)}, bf16[26,1,128,128]{3,2,1,0:T(8,128)(2,1)}, u32[]{:S(2)}, u32[]{:S(2)}) collective-permute-start(bf16[26,1,128,128]{3,2,1,0:T(8,128)(2,1)} %broadcast_select_fusion.6), channel_id=1, source_target_pairs={{1,0},{2,1},{3,2},{4,3},{5,4},{6,5},{7,6},{8,7},{9,8},{10,9},{11,1... | collective-permute-start | bytes 2555912 | tf_op jit(solution)/shard_map/ppermute | solution.py:17
  69.3 13.9 %collective-permute-done.3 = bf16[26,1,128,128]{3,2,1,0:T(8,128)(2,1)} collective-permute-done((bf16[26,1,128,128]{3,2,1,0:T(8,128)(2,1)}, bf16[26,1,128,128]{3,2,1,0:T(8,128)(2,1)}, u32[]{:S(2)}, u32[]{:S(2)}) %collective-permute-start.3) | collective-permute-done | bytes 852000 | tf_op jit(solution)/shard_map/ppermute | solution.py:14
  83.2 3.1 fusion.35
  86.4 3.1 fusion.39
  89.5 6.9 fusion.26
  98.6 12.1 %collective-permute-done.5 = bf16[26,1,128,128]{3,2,1,0:T(8,128)(2,1)S(1)} collective-permute-done((bf16[26,1,128,128]{3,2,1,0:T(8,128)(2,1)S(1)}, bf16[26,1,128,128]{3,2,1,0:T(8,128)(2,1)S(1)}, u32[]{:S(2)}, u32[]{:S(2)}) %collective-permute-start.5) | collective-permute-done | bytes 852000 | tf_op jit(solution)/shard_map/ppermute | solution.py:25
  113.6 7.4 %collective-permute-start.7 = (bf16[26,1,128,128]{3,2,1,0:T(8,128)(2,1)}, bf16[26,1,128,128]{3,2,1,0:T(8,128)(2,1)}, u32[]{:S(2)}, u32[]{:S(2)}) collective-permute-start(bf16[26,1,128,128]{3,2,1,0:T(8,128)(2,1)} %broadcast_select_fusion.5), channel_id=1, source_target_pairs={{1,0},{2,1},{3,2},{4,3},{5,4},{6,5},{7,6},{8,7},{9,8},{10,9},{11,1... | collective-permute-start | bytes 2555912 | tf_op jit(solution)/shard_map/ppermute | solution.py:17
  123.0 14.0 %collective-permute-done.6 = bf16[26,1,128,128]{3,2,1,0:T(8,128)(2,1)} collective-permute-done((bf16[26,1,128,128]{3,2,1,0:T(8,128)(2,1)}, bf16[26,1,128,128]{3,2,1,0:T(8,128)(2,1)}, u32[]{:S(2)}, u32[]{:S(2)}) %collective-permute-start.6) | collective-permute-done | bytes 852000 | tf_op jit(solution)/shard_map/ppermute | solution.py:14
  137.0 3.1 fusion.41
  140.2 3.1 fusion.45
  143.3 6.9 fusion.25
  152.4 12.1 %collective-permute-done.8 = bf16[26,1,128,128]{3,2,1,0:T(8,128)(2,1)S(1)} collective-permute-done((bf16[26,1,128,128]{3,2,1,0:T(8,128)(2,1)S(1)}, bf16[26,1,128,128]{3,2,1,0:T(8,128)(2,1)S(1)}, u32[]{:S(2)}, u32[]{:S(2)}) %collective-permute-start.8) | collective-permute-done | bytes 852000 | tf_op jit(solution)/shard_map/ppermute | solution.py:25
  167.4 7.5 %collective-permute-start.10 = (bf16[26,1,128,128]{3,2,1,0:T(8,128)(2,1)}, bf16[26,1,128,128]{3,2,1,0:T(8,128)(2,1)}, u32[]{:S(2)}, u32[]{:S(2)}) collective-permute-start(bf16[26,1,128,128]{3,2,1,0:T(8,128)(2,1)} %broadcast_select_fusion.4), channel_id=1, source_target_pairs={{1,0},{2,1},{3,2},{4,3},{5,4},{6,5},{7,6},{8,7},{9,8},{10,9},{11,1... | collective-permute-start | bytes 2555912 | tf_op jit(solution)/shard_map/ppermute | solution.py:17
  176.8 10.6 %collective-permute-done.9 = bf16[26,1,128,128]{3,2,1,0:T(8,128)(2,1)} collective-permute-done((bf16[26,1,128,128]{3,2,1,0:T(8,128)(2,1)}, bf16[26,1,128,128]{3,2,1,0:T(8,128)(2,1)}, u32[]{:S(2)}, u32[]{:S(2)}) %collective-permute-start.9) | collective-permute-done | bytes 852000 | tf_op jit(solution)/shard_map/ppermute | solution.py:14
  187.4 3.1 fusion.47
  190.6 3.1 fusion.51
  193.7 6.9 fusion.24
  202.8 12.1 %collective-permute-done.11 = bf16[26,1,128,128]{3,2,1,0:T(8,128)(2,1)S(1)} collective-permute-done((bf16[26,1,128,128]{3,2,1,0:T(8,128)(2,1)S(1)}, bf16[26,1,128,128]{3,2,1,0:T(8,128)(2,1)S(1)}, u32[]{:S(2)}, u32[]{:S(2)}) %collective-permute-start.11) | collective-permute-done | bytes 852000 | tf_op jit(solution)/shard_map/ppermute | solution.py:25
  217.8 7.5 %collective-permute-start.13 = (bf16[26,1,128,128]{3,2,1,0:T(8,128)(2,1)}, bf16[26,1,128,128]{3,2,1,0:T(8,128)(2,1)}, u32[]{:S(2)}, u32[]{:S(2)}) collective-permute-start(bf16[26,1,128,128]{3,2,1,0:T(8,128)(2,1)} %broadcast_select_fusion.3), channel_id=1, source_target_pairs={{1,0},{2,1},{3,2},{4,3},{5,4},{6,5},{7,6},{8,7},{9,8},{10,9},{11,1... | collective-permute-start | bytes 2555912 | tf_op jit(solution)/shard_map/ppermute | solution.py:17
  227.3 7.1 %collective-permute-done.12 = bf16[26,1,128,128]{3,2,1,0:T(8,128)(2,1)} collective-permute-done((bf16[26,1,128,128]{3,2,1,0:T(8,128)(2,1)}, bf16[26,1,128,128]{3,2,1,0:T(8,128)(2,1)}, u32[]{:S(2)}, u32[]{:S(2)}) %collective-permute-start.12) | collective-permute-done | bytes 852000 | tf_op jit(solution)/shard_map/ppermute | solution.py:14
  234.4 3.1 fusion.53
  237.6 3.1 fusion.57
  240.7 6.9 fusion.23
  249.9 12.1 %collective-permute-done.14 = bf16[26,1,128,128]{3,2,1,0:T(8,128)(2,1)S(1)} collective-permute-done((bf16[26,1,128,128]{3,2,1,0:T(8,128)(2,1)S(1)}, bf16[26,1,128,128]{3,2,1,0:T(8,128)(2,1)S(1)}, u32[]{:S(2)}, u32[]{:S(2)}) %collective-permute-start.14) | collective-permute-done | bytes 852000 | tf_op jit(solution)/shard_map/ppermute | solution.py:25
  264.9 7.7 %collective-permute-start.16 = (bf16[26,1,128,128]{3,2,1,0:T(8,128)(2,1)}, bf16[26,1,128,128]{3,2,1,0:T(8,128)(2,1)}, u32[]{:S(2)}, u32[]{:S(2)}) collective-permute-start(bf16[26,1,128,128]{3,2,1,0:T(8,128)(2,1)} %broadcast_select_fusion.2), channel_id=1, source_target_pairs={{1,0},{2,1},{3,2},{4,3},{5,4},{6,5},{7,6},{8,7},{9,8},{10,9},{11,1... | collective-permute-start | bytes 2555912 | tf_op jit(solution)/shard_map/ppermute | solution.py:17
  274.5 6.6 collective-permute-done.15
  281.2 3.1 fusion.59
  284.3 3.1 fusion.63
  287.4 6.9 fusion.22
  296.6 12.1 %collective-permute-done.17 = bf16[26,1,128,128]{3,2,1,0:T(8,128)(2,1)S(1)} collective-permute-done((bf16[26,1,128,128]{3,2,1,0:T(8,128)(2,1)S(1)}, bf16[26,1,128,128]{3,2,1,0:T(8,128)(2,1)S(1)}, u32[]{:S(2)}, u32[]{:S(2)}) %collective-permute-start.17) | collective-permute-done | bytes 852000 | tf_op jit(solution)/shard_map/ppermute | solution.py:25
  311.6 7.4 %collective-permute-start.19 = (bf16[26,1,128,128]{3,2,1,0:T(8,128)(2,1)}, bf16[26,1,128,128]{3,2,1,0:T(8,128)(2,1)}, u32[]{:S(2)}, u32[]{:S(2)}) collective-permute-start(bf16[26,1,128,128]{3,2,1,0:T(8,128)(2,1)} %broadcast_select_fusion.1), channel_id=1, source_target_pairs={{1,0},{2,1},{3,2},{4,3},{5,4},{6,5},{7,6},{8,7},{9,8},{10,9},{11,1... | collective-permute-start | bytes 2555912 | tf_op jit(solution)/shard_map/ppermute | solution.py:17
  321.0 6.9 collective-permute-done.18
  327.9 3.1 fusion.65
  331.0 3.1 fusion.69
  334.2 6.9 fusion.21
  346.0 7.2 %collective-permute-start.22 = (bf16[1,128,128]{2,1,0:T(8,128)(2,1)S(1)}, bf16[1,128,128]{2,1,0:T(8,128)(2,1)S(1)}, u32[]{:S(2)}, u32[]{:S(2)}) collective-permute-start(bf16[1,128,128]{2,1,0:T(8,128)(2,1)S(1)} %fusion.144), channel_id=1, source_target_pairs={{1,0},{2,1},{3,2},{4,3},{5,4},{6,5},{7,6},{8,7},{9,8},{10,9},{11,1... | collective-permute-start | bytes 98312 | tf_op jit(solution)/shard_map/ppermute | solution.py:17
  356.9 75.2 %psum.28 = f32[]{:T(128)} all-reduce(f32[]{:T(128)} %get-tuple-element.6), channel_id=1, replica_groups=mesh['sec'=8,'blk'=32] {'blk'}, use_global_device_ids=true, to_apply=%region_1.2 | all-reduce | flops 1 | bytes 8 | tf_op jit(solution)/shard_map/psum | solution.py:78
  434.7 7.2 %collective-permute-start.24 = (bf16[1,128,128]{2,1,0:T(8,128)(2,1)S(1)}, bf16[1,128,128]{2,1,0:T(8,128)(2,1)S(1)}, u32[]{:S(2)}, u32[]{:S(2)}) collective-permute-start(bf16[1,128,128]{2,1,0:T(8,128)(2,1)S(1)} %divide_convert_fusion.2), channel_id=1, source_target_pairs={{1,0},{2,1},{3,2},{4,3},{5,4},{6,5},{7,6},{8,7},{9,8},{10,9},{11,1... | collective-permute-start | bytes 98312 | tf_op jit(solution)/shard_map/ppermute | solution.py:17
  444.7 75.9 %psum.29 = f32[]{:T(128)} all-reduce(f32[]{:T(128)} %get-tuple-element.8), channel_id=1, replica_groups=mesh['sec'=8,'blk'=32] {'blk'}, use_global_device_ids=true, to_apply=%region_3.4 | all-reduce | flops 1 | bytes 8 | tf_op jit(solution)/shard_map/psum | solution.py:78
  523.3 7.2 %collective-permute-start.26 = (bf16[1,128,128]{2,1,0:T(8,128)(2,1)S(1)}, bf16[1,128,128]{2,1,0:T(8,128)(2,1)S(1)}, u32[]{:S(2)}, u32[]{:S(2)}) collective-permute-start(bf16[1,128,128]{2,1,0:T(8,128)(2,1)S(1)} %divide_convert_fusion.1), channel_id=1, source_target_pairs={{1,0},{2,1},{3,2},{4,3},{5,4},{6,5},{7,6},{8,7},{9,8},{10,9},{11,1... | collective-permute-start | bytes 98312 | tf_op jit(solution)/shard_map/ppermute | solution.py:17
  533.4 75.9 %psum.30 = f32[]{:T(128)} all-reduce(f32[]{:T(128)} %get-tuple-element.10), channel_id=1, replica_groups=mesh['sec'=8,'blk'=32] {'blk'}, use_global_device_ids=true, to_apply=%region_5.6 | all-reduce | flops 1 | bytes 8 | tf_op jit(solution)/shard_map/psum | solution.py:78
  611.9 7.2 %collective-permute-start.28 = (bf16[1,128,128]{2,1,0:T(8,128)(2,1)S(1)}, bf16[1,128,128]{2,1,0:T(8,128)(2,1)S(1)}, u32[]{:S(2)}, u32[]{:S(2)}) collective-permute-start(bf16[1,128,128]{2,1,0:T(8,128)(2,1)S(1)} %divide_convert_fusion), channel_id=1, source_target_pairs={{1,0},{2,1},{3,2},{4,3},{5,4},{6,5},{7,6},{8,7},{9,8},{10,9},{11,1... | collective-permute-start | bytes 98312 | tf_op jit(solution)/shard_map/ppermute | solution.py:17
  621.9 75.9 %psum.31 = f32[]{:T(128)} all-reduce(f32[]{:T(128)} %get-tuple-element.12), channel_id=1, replica_groups=mesh['sec'=8,'blk'=32] {'blk'}, use_global_device_ids=true, to_apply=%region_7.8 | all-reduce | flops 1 | bytes 8 | tf_op jit(solution)/shard_map/psum | solution.py:78
  (79 shorter events, 74.6 us)
Async XLA Ops:
  0.6 354.9 %copy-start = (bf16[1,26,1,128,128]{4,3,2,1,0:T(8,128)(2,1)S(1)}, bf16[1,26,1,128,128]{4,3,2,1,0:T(8,128)(2,1)}, u32[]{:S(2)}) copy-start(bf16[1,26,1,128,128]{4,3,2,1,0:T(8,128)(2,1)} %param.9) | copy-start | bytes 2555908
  0.6 11.5 %copy-start.1 = (bf16[26,1,128,128]{3,2,1,0:T(8,128)(2,1)S(1)}, bf16[26,1,128,128]{3,2,1,0:T(8,128)(2,1)}, u32[]{:S(2)}) copy-start(bf16[26,1,128,128]{3,2,1,0:T(8,128)(2,1)} %param.6) | copy-start | bytes 2555908
  0.7 11.5 %copy-start.3 = (bf16[1,1,3,128,128]{4,3,2,1,0:T(8,128)(2,1)S(1)}, bf16[1,1,3,128,128]{4,3,2,1,0:T(8,128)(2,1)}, u32[]{:S(2)}) copy-start(bf16[1,1,3,128,128]{4,3,2,1,0:T(8,128)(2,1)} %param.7) | copy-start | bytes 294916
  3.0 26.2 %collective-permute-start = (bf16[26,1,128,128]{2,3,0,1:T(8,128)(2,1)}, bf16[26,1,128,128]{2,3,0,1:T(8,128)(2,1)}, u32[]{:S(2)}, u32[]{:S(2)}) collective-permute-start(bf16[26,1,128,128]{2,3,0,1:T(8,128)(2,1)} %copy.49), channel_id=1, source_target_pairs={{0,1},{1,2},{2,3},{3,4},{4,5},{5,6},{6,7},{7,8},{8,9},{9,10},{10,1... | collective-permute-start | bytes 2555912 | tf_op jit(solution)/shard_map/ppermute | solution.py:14
  6.4 25.9 %collective-permute-start.1 = (bf16[26,1,128,128]{2,3,0,1:T(8,128)(2,1)}, bf16[26,1,128,128]{2,3,0,1:T(8,128)(2,1)}, u32[]{:S(2)}, u32[]{:S(2)}) collective-permute-start(bf16[26,1,128,128]{2,3,0,1:T(8,128)(2,1)} %copy.49), channel_id=1, source_target_pairs={{1,0},{2,1},{3,2},{4,3},{5,4},{6,5},{7,6},{8,7},{9,8},{10,9},{11,1... | collective-permute-start | bytes 2555912 | tf_op jit(solution)/shard_map/ppermute | solution.py:17
  32.3 3.1 copy-start.4
  42.6 14.0 %collective-permute-start.2 = (bf16[26,1,128,128]{3,2,1,0:T(8,128)(2,1)S(1)}, bf16[26,1,128,128]{3,2,1,0:T(8,128)(2,1)S(1)}, u32[]{:S(2)}, u32[]{:S(2)}) collective-permute-start(bf16[26,1,128,128]{3,2,1,0:T(8,128)(2,1)S(1)} %copy.52), channel_id=1, source_target_pairs={{0,32},{32,64},{64,96},{96,128},{128,160},{160,192},{192,224},{1,3... | collective-permute-start | bytes 2555912 | tf_op jit(solution)/shard_map/ppermute | solution.py:25
  57.6 25.6 %collective-permute-start.3 = (bf16[26,1,128,128]{3,2,1,0:T(8,128)(2,1)}, bf16[26,1,128,128]{3,2,1,0:T(8,128)(2,1)}, u32[]{:S(2)}, u32[]{:S(2)}) collective-permute-start(bf16[26,1,128,128]{3,2,1,0:T(8,128)(2,1)} %broadcast_select_fusion.6), channel_id=1, source_target_pairs={{0,1},{1,2},{2,3},{3,4},{4,5},{5,6},{6,7},{7,8},{8,9},{9,10},{10,1... | collective-permute-start | bytes 2555912 | tf_op jit(solution)/shard_map/ppermute | solution.py:14
  59.5 26.8 %collective-permute-start.4 = (bf16[26,1,128,128]{3,2,1,0:T(8,128)(2,1)}, bf16[26,1,128,128]{3,2,1,0:T(8,128)(2,1)}, u32[]{:S(2)}, u32[]{:S(2)}) collective-permute-start(bf16[26,1,128,128]{3,2,1,0:T(8,128)(2,1)} %broadcast_select_fusion.6), channel_id=1, source_target_pairs={{1,0},{2,1},{3,2},{4,3},{5,4},{6,5},{7,6},{8,7},{9,8},{10,9},{11,1... | collective-permute-start | bytes 2555912 | tf_op jit(solution)/shard_map/ppermute | solution.py:17
  96.7 14.0 %collective-permute-start.5 = (bf16[26,1,128,128]{3,2,1,0:T(8,128)(2,1)S(1)}, bf16[26,1,128,128]{3,2,1,0:T(8,128)(2,1)S(1)}, u32[]{:S(2)}, u32[]{:S(2)}) collective-permute-start(bf16[26,1,128,128]{3,2,1,0:T(8,128)(2,1)S(1)} %copy.56), channel_id=1, source_target_pairs={{0,32},{32,64},{64,96},{96,128},{128,160},{160,192},{192,224},{1,3... | collective-permute-start | bytes 2555912 | tf_op jit(solution)/shard_map/ppermute | solution.py:25
  111.7 25.3 %collective-permute-start.6 = (bf16[26,1,128,128]{3,2,1,0:T(8,128)(2,1)}, bf16[26,1,128,128]{3,2,1,0:T(8,128)(2,1)}, u32[]{:S(2)}, u32[]{:S(2)}) collective-permute-start(bf16[26,1,128,128]{3,2,1,0:T(8,128)(2,1)} %broadcast_select_fusion.5), channel_id=1, source_target_pairs={{0,1},{1,2},{2,3},{3,4},{4,5},{5,6},{6,7},{7,8},{8,9},{9,10},{10,1... | collective-permute-start | bytes 2555912 | tf_op jit(solution)/shard_map/ppermute | solution.py:14
  113.6 26.5 %collective-permute-start.7 = (bf16[26,1,128,128]{3,2,1,0:T(8,128)(2,1)}, bf16[26,1,128,128]{3,2,1,0:T(8,128)(2,1)}, u32[]{:S(2)}, u32[]{:S(2)}) collective-permute-start(bf16[26,1,128,128]{3,2,1,0:T(8,128)(2,1)} %broadcast_select_fusion.5), channel_id=1, source_target_pairs={{1,0},{2,1},{3,2},{4,3},{5,4},{6,5},{7,6},{8,7},{9,8},{10,9},{11,1... | collective-permute-start | bytes 2555912 | tf_op jit(solution)/shard_map/ppermute | solution.py:17
  150.5 14.0 %collective-permute-start.8 = (bf16[26,1,128,128]{3,2,1,0:T(8,128)(2,1)S(1)}, bf16[26,1,128,128]{3,2,1,0:T(8,128)(2,1)S(1)}, u32[]{:S(2)}, u32[]{:S(2)}) collective-permute-start(bf16[26,1,128,128]{3,2,1,0:T(8,128)(2,1)S(1)} %copy.60), channel_id=1, source_target_pairs={{0,32},{32,64},{64,96},{96,128},{128,160},{160,192},{192,224},{1,3... | collective-permute-start | bytes 2555912 | tf_op jit(solution)/shard_map/ppermute | solution.py:25
  165.5 21.9 %collective-permute-start.9 = (bf16[26,1,128,128]{3,2,1,0:T(8,128)(2,1)}, bf16[26,1,128,128]{3,2,1,0:T(8,128)(2,1)}, u32[]{:S(2)}, u32[]{:S(2)}) collective-permute-start(bf16[26,1,128,128]{3,2,1,0:T(8,128)(2,1)} %broadcast_select_fusion.4), channel_id=1, source_target_pairs={{0,1},{1,2},{2,3},{3,4},{4,5},{5,6},{6,7},{7,8},{8,9},{9,10},{10,1... | collective-permute-start | bytes 2555912 | tf_op jit(solution)/shard_map/ppermute | solution.py:14
  167.4 23.1 %collective-permute-start.10 = (bf16[26,1,128,128]{3,2,1,0:T(8,128)(2,1)}, bf16[26,1,128,128]{3,2,1,0:T(8,128)(2,1)}, u32[]{:S(2)}, u32[]{:S(2)}) collective-permute-start(bf16[26,1,128,128]{3,2,1,0:T(8,128)(2,1)} %broadcast_select_fusion.4), channel_id=1, source_target_pairs={{1,0},{2,1},{3,2},{4,3},{5,4},{6,5},{7,6},{8,7},{9,8},{10,9},{11,1... | collective-permute-start | bytes 2555912 | tf_op jit(solution)/shard_map/ppermute | solution.py:17
  200.9 14.0 %collective-permute-start.11 = (bf16[26,1,128,128]{3,2,1,0:T(8,128)(2,1)S(1)}, bf16[26,1,128,128]{3,2,1,0:T(8,128)(2,1)S(1)}, u32[]{:S(2)}, u32[]{:S(2)}) collective-permute-start(bf16[26,1,128,128]{3,2,1,0:T(8,128)(2,1)S(1)} %copy.64), channel_id=1, source_target_pairs={{0,32},{32,64},{64,96},{96,128},{128,160},{160,192},{192,224},{1,3... | collective-permute-start | bytes 2555912 | tf_op jit(solution)/shard_map/ppermute | solution.py:25
  215.9 18.5 %collective-permute-start.12 = (bf16[26,1,128,128]{3,2,1,0:T(8,128)(2,1)}, bf16[26,1,128,128]{3,2,1,0:T(8,128)(2,1)}, u32[]{:S(2)}, u32[]{:S(2)}) collective-permute-start(bf16[26,1,128,128]{3,2,1,0:T(8,128)(2,1)} %broadcast_select_fusion.3), channel_id=1, source_target_pairs={{0,1},{1,2},{2,3},{3,4},{4,5},{5,6},{6,7},{7,8},{8,9},{9,10},{10,1... | collective-permute-start | bytes 2555912 | tf_op jit(solution)/shard_map/ppermute | solution.py:14
  217.8 19.7 %collective-permute-start.13 = (bf16[26,1,128,128]{3,2,1,0:T(8,128)(2,1)}, bf16[26,1,128,128]{3,2,1,0:T(8,128)(2,1)}, u32[]{:S(2)}, u32[]{:S(2)}) collective-permute-start(bf16[26,1,128,128]{3,2,1,0:T(8,128)(2,1)} %broadcast_select_fusion.3), channel_id=1, source_target_pairs={{1,0},{2,1},{3,2},{4,3},{5,4},{6,5},{7,6},{8,7},{9,8},{10,9},{11,1... | collective-permute-start | bytes 2555912 | tf_op jit(solution)/shard_map/ppermute | solution.py:17
  247.9 14.0 %collective-permute-start.14 = (bf16[26,1,128,128]{3,2,1,0:T(8,128)(2,1)S(1)}, bf16[26,1,128,128]{3,2,1,0:T(8,128)(2,1)S(1)}, u32[]{:S(2)}, u32[]{:S(2)}) collective-permute-start(bf16[26,1,128,128]{3,2,1,0:T(8,128)(2,1)S(1)} %copy.68), channel_id=1, source_target_pairs={{0,32},{32,64},{64,96},{96,128},{128,160},{160,192},{192,224},{1,3... | collective-permute-start | bytes 2555912 | tf_op jit(solution)/shard_map/ppermute | solution.py:25
  262.9 18.2 %collective-permute-start.15 = (bf16[26,1,128,128]{3,2,1,0:T(8,128)(2,1)}, bf16[26,1,128,128]{3,2,1,0:T(8,128)(2,1)}, u32[]{:S(2)}, u32[]{:S(2)}) collective-permute-start(bf16[26,1,128,128]{3,2,1,0:T(8,128)(2,1)} %broadcast_select_fusion.2), channel_id=1, source_target_pairs={{0,1},{1,2},{2,3},{3,4},{4,5},{5,6},{6,7},{7,8},{8,9},{9,10},{10,1... | collective-permute-start | bytes 2555912 | tf_op jit(solution)/shard_map/ppermute | solution.py:14
  264.9 19.4 %collective-permute-start.16 = (bf16[26,1,128,128]{3,2,1,0:T(8,128)(2,1)}, bf16[26,1,128,128]{3,2,1,0:T(8,128)(2,1)}, u32[]{:S(2)}, u32[]{:S(2)}) collective-permute-start(bf16[26,1,128,128]{3,2,1,0:T(8,128)(2,1)} %broadcast_select_fusion.2), channel_id=1, source_target_pairs={{1,0},{2,1},{3,2},{4,3},{5,4},{6,5},{7,6},{8,7},{9,8},{10,9},{11,1... | collective-permute-start | bytes 2555912 | tf_op jit(solution)/shard_map/ppermute | solution.py:17
  294.7 14.0 %collective-permute-start.17 = (bf16[26,1,128,128]{3,2,1,0:T(8,128)(2,1)S(1)}, bf16[26,1,128,128]{3,2,1,0:T(8,128)(2,1)S(1)}, u32[]{:S(2)}, u32[]{:S(2)}) collective-permute-start(bf16[26,1,128,128]{3,2,1,0:T(8,128)(2,1)S(1)} %copy.72), channel_id=1, source_target_pairs={{0,32},{32,64},{64,96},{96,128},{128,160},{160,192},{192,224},{1,3... | collective-permute-start | bytes 2555912 | tf_op jit(solution)/shard_map/ppermute | solution.py:25
  309.7 18.2 %collective-permute-start.18 = (bf16[26,1,128,128]{3,2,1,0:T(8,128)(2,1)}, bf16[26,1,128,128]{3,2,1,0:T(8,128)(2,1)}, u32[]{:S(2)}, u32[]{:S(2)}) collective-permute-start(bf16[26,1,128,128]{3,2,1,0:T(8,128)(2,1)} %broadcast_select_fusion.1), channel_id=1, source_target_pairs={{0,1},{1,2},{2,3},{3,4},{4,5},{5,6},{6,7},{7,8},{8,9},{9,10},{10,1... | collective-permute-start | bytes 2555912 | tf_op jit(solution)/shard_map/ppermute | solution.py:14
  311.6 19.4 %collective-permute-start.19 = (bf16[26,1,128,128]{3,2,1,0:T(8,128)(2,1)}, bf16[26,1,128,128]{3,2,1,0:T(8,128)(2,1)}, u32[]{:S(2)}, u32[]{:S(2)}) collective-permute-start(bf16[26,1,128,128]{3,2,1,0:T(8,128)(2,1)} %broadcast_select_fusion.1), channel_id=1, source_target_pairs={{1,0},{2,1},{3,2},{4,3},{5,4},{6,5},{7,6},{8,7},{9,8},{10,9},{11,1... | collective-permute-start | bytes 2555912 | tf_op jit(solution)/shard_map/ppermute | solution.py:17
  341.0 2.9 copy-start.5
  341.4 14.0 %collective-permute-start.20 = (bf16[26,1,128,128]{3,2,1,0:T(8,128)(2,1)S(1)}, bf16[26,1,128,128]{3,2,1,0:T(8,128)(2,1)S(1)}, u32[]{:S(2)}, u32[]{:S(2)}) collective-permute-start(bf16[26,1,128,128]{3,2,1,0:T(8,128)(2,1)S(1)} %copy.76), channel_id=1, source_target_pairs={{0,32},{32,64},{64,96},{96,128},{128,160},{160,192},{192,224},{1,3... | collective-permute-start | bytes 2555912 | tf_op jit(solution)/shard_map/ppermute | solution.py:25
  344.1 11.4 %collective-permute-start.21 = (bf16[1,128,128]{2,1,0:T(8,128)(2,1)S(1)}, bf16[1,128,128]{2,1,0:T(8,128)(2,1)S(1)}, u32[]{:S(2)}, u32[]{:S(2)}) collective-permute-start(bf16[1,128,128]{2,1,0:T(8,128)(2,1)S(1)} %fusion.144), channel_id=1, source_target_pairs={{0,1},{1,2},{2,3},{3,4},{4,5},{5,6},{6,7},{7,8},{8,9},{9,10},{10,1... | collective-permute-start | bytes 98312 | tf_op jit(solution)/shard_map/ppermute | solution.py:14
  346.0 9.5 %collective-permute-start.22 = (bf16[1,128,128]{2,1,0:T(8,128)(2,1)S(1)}, bf16[1,128,128]{2,1,0:T(8,128)(2,1)S(1)}, u32[]{:S(2)}, u32[]{:S(2)}) collective-permute-start(bf16[1,128,128]{2,1,0:T(8,128)(2,1)S(1)} %fusion.144), channel_id=1, source_target_pairs={{1,0},{2,1},{3,2},{4,3},{5,4},{6,5},{7,6},{8,7},{9,8},{10,9},{11,1... | collective-permute-start | bytes 98312 | tf_op jit(solution)/shard_map/ppermute | solution.py:17
  355.5 265.2 %copy-start.2 = (bf16[26,1,128,128]{3,2,1,0:T(8,128)(2,1)}, bf16[26,1,128,128]{3,2,1,0:T(8,128)(2,1)S(1)}, u32[]{:S(2)}) copy-start(bf16[26,1,128,128]{3,2,1,0:T(8,128)(2,1)S(1)} %broadcast_select_fusion) | copy-start | bytes 2555908
  432.7 9.2 %collective-permute-start.23 = (bf16[1,128,128]{2,1,0:T(8,128)(2,1)S(1)}, bf16[1,128,128]{2,1,0:T(8,128)(2,1)S(1)}, u32[]{:S(2)}, u32[]{:S(2)}) collective-permute-start(bf16[1,128,128]{2,1,0:T(8,128)(2,1)S(1)} %divide_convert_fusion.2), channel_id=1, source_target_pairs={{0,1},{1,2},{2,3},{3,4},{4,5},{5,6},{6,7},{7,8},{8,9},{9,10},{10,1... | collective-permute-start | bytes 98312 | tf_op jit(solution)/shard_map/ppermute | solution.py:14
  434.7 8.8 %collective-permute-start.24 = (bf16[1,128,128]{2,1,0:T(8,128)(2,1)S(1)}, bf16[1,128,128]{2,1,0:T(8,128)(2,1)S(1)}, u32[]{:S(2)}, u32[]{:S(2)}) collective-permute-start(bf16[1,128,128]{2,1,0:T(8,128)(2,1)S(1)} %divide_convert_fusion.2), channel_id=1, source_target_pairs={{1,0},{2,1},{3,2},{4,3},{5,4},{6,5},{7,6},{8,7},{9,8},{10,9},{11,1... | collective-permute-start | bytes 98312 | tf_op jit(solution)/shard_map/ppermute | solution.py:17
  521.4 9.2 %collective-permute-start.25 = (bf16[1,128,128]{2,1,0:T(8,128)(2,1)S(1)}, bf16[1,128,128]{2,1,0:T(8,128)(2,1)S(1)}, u32[]{:S(2)}, u32[]{:S(2)}) collective-permute-start(bf16[1,128,128]{2,1,0:T(8,128)(2,1)S(1)} %divide_convert_fusion.1), channel_id=1, source_target_pairs={{0,1},{1,2},{2,3},{3,4},{4,5},{5,6},{6,7},{7,8},{8,9},{9,10},{10,1... | collective-permute-start | bytes 98312 | tf_op jit(solution)/shard_map/ppermute | solution.py:14
  523.3 8.8 %collective-permute-start.26 = (bf16[1,128,128]{2,1,0:T(8,128)(2,1)S(1)}, bf16[1,128,128]{2,1,0:T(8,128)(2,1)S(1)}, u32[]{:S(2)}, u32[]{:S(2)}) collective-permute-start(bf16[1,128,128]{2,1,0:T(8,128)(2,1)S(1)} %divide_convert_fusion.1), channel_id=1, source_target_pairs={{1,0},{2,1},{3,2},{4,3},{5,4},{6,5},{7,6},{8,7},{9,8},{10,9},{11,1... | collective-permute-start | bytes 98312 | tf_op jit(solution)/shard_map/ppermute | solution.py:17
  610.0 9.2 %collective-permute-start.27 = (bf16[1,128,128]{2,1,0:T(8,128)(2,1)S(1)}, bf16[1,128,128]{2,1,0:T(8,128)(2,1)S(1)}, u32[]{:S(2)}, u32[]{:S(2)}) collective-permute-start(bf16[1,128,128]{2,1,0:T(8,128)(2,1)S(1)} %divide_convert_fusion), channel_id=1, source_target_pairs={{0,1},{1,2},{2,3},{3,4},{4,5},{5,6},{6,7},{7,8},{8,9},{9,10},{10,1... | collective-permute-start | bytes 98312 | tf_op jit(solution)/shard_map/ppermute | solution.py:14
  611.9 8.8 %collective-permute-start.28 = (bf16[1,128,128]{2,1,0:T(8,128)(2,1)S(1)}, bf16[1,128,128]{2,1,0:T(8,128)(2,1)S(1)}, u32[]{:S(2)}, u32[]{:S(2)}) collective-permute-start(bf16[1,128,128]{2,1,0:T(8,128)(2,1)S(1)} %divide_convert_fusion), channel_id=1, source_target_pairs={{1,0},{2,1},{3,2},{4,3},{5,4},{6,5},{7,6},{8,7},{9,8},{10,9},{11,1... | collective-permute-start | bytes 98312 | tf_op jit(solution)/shard_map/ppermute | solution.py:17
where the time goes:
time: 707 us; the launch traced here: 699 us
  blocking collectives  303 us (43%)
  waiting for transfers between devices  155 us (22%)
  starting transfers between devices  116 us (16%)
  matrix products  110 us (16%)
    psum x4, blocking collectives, per_device(): total = lax.psum(jnp.sum(psi * psi), 'blk')  303 us
    ppermute x11, starting transfers between devices, padded_2(): lax.ppermute(lax.slice_in_dim(block, 0, width, axis=dim), axis, backward)  80 us
    ppermute x11, waiting for transfers between devices, padded_2(): lax.ppermute(lax.slice_in_dim(block, block.shape[dim] - width, None, axis...  75.4 us
    ppermute x7, waiting for transfers between devices, shifted(): lax.ppermute(value, axis, [(source, source + steps) for source in range(l...  74.6 us
    dot_general x21, matrix products, padded_step(): jnp.einsum('wqik,qkl->wqil', left, tensor, preferred_element_type=jnp.flo...  56.3 us
    dot_general x7, matrix products, apply_mix(): jnp.einsum('vw,wqil->vqil', mix, total, precision=lax.Precision.HIGHEST)  48.1 us
    ppermute x11, starting transfers between devices, padded_2(): lax.ppermute(lax.slice_in_dim(block, block.shape[dim] - width, None, axis...  22.5 us
  transfers between devices with their start and end apart: 29, of which 17 were waited for; matrix products, arithmetic and copies ran while one was open for 5% of the time, Pallas kernels for 0%

commit v1 on v0

v1 whole, which is shorter than its diff:
```python
import jax
import jax.numpy as jnp
from jax import lax
from jax.experimental import pallas as pl
from jax.experimental.pallas import tpu as pltpu
from jax.sharding import PartitionSpec as P

ITERS = 4
B = 128
WM = 26
NS = 8
NQ = 32
SLOTS = 4
STEPS = NS - 1
PAIRS = WM // 2
ROWS = 16
KR = WM * ROWS
MESH = pl.DeviceIdType.MESH
F32 = jnp.float32
BF16 = jnp.bfloat16


def dot(a, b):
    return jnp.dot(a, b, preferred_element_type=F32)


def kernel(
    env_hbm, trans, mix, renv_hbm, start, rank, state, env_out,
    raw, halo_l, halo_r, recv, envm, renv, tall, tt, mixall, amat, own_mix,
    xsend, xl, xr, psend, pall,
    load_sem, renv_sem, out_sem, recv_sem, deliver_sem, local_sem,
    hrecv, hsend, trecv, tsend, fsend, mrecv, msend,
    xrecv, xsem, precv, psem,
):
    g = lax.axis_index("sec")
    q = lax.axis_index("blk")
    y = g // 2
    core = lax.rem(g, 2)
    right = lax.rem(q + 1, NQ)
    left = lax.rem(q + NQ - 1, NQ)
    first = 3 * g + jnp.where(g >= 1, 1, 0) + jnp.where(g >= 3, 1, 0)
    four = jnp.logical_or(g == 0, g == 2)

    barrier = pltpu.get_barrier_semaphore()

    def greet_sec(i, carry):
        pl.semaphore_signal(barrier, inc=1, device_id=(lax.rem(g + i, NS), q), device_id_type=MESH)
        return carry

    def greet_blk(i, carry):
        pl.semaphore_signal(barrier, inc=1, device_id=(g, lax.rem(q + i, NQ)), device_id_type=MESH)
        return carry

    lax.fori_loop(1, NS, greet_sec, 0)
    lax.fori_loop(1, NQ, greet_blk, 0)

    def each_slot(j, body):
        if j < SLOTS - 1:
            body()
        else:
            pl.when(four)(body)

    def load(j):
        return pltpu.make_async_copy(env_hbm.at[first + j], raw.at[0, j], load_sem.at[j])

    for j in range(SLOTS):
        each_slot(j, lambda j=j: load(j).start())

    @pl.when(g == 0)
    def _():
        def body(w, carry):
            pltpu.make_async_copy(env_hbm.at[w], recv.at[w], recv_sem.at[w]).start()
            return carry

        lax.fori_loop(0, WM, body, 0)

    renv_copy = pltpu.make_async_copy(renv_hbm, renv, renv_sem)
    renv_copy.start()

    own_mix[...] = jnp.zeros_like(own_mix)
    own_mix[:WM, :WM] = mix[...]
    tall[g] = trans[...]
    mixall[g] = own_mix[...]
    row = lax.broadcasted_iota(jnp.int32, (32, B), 0)
    col = lax.broadcasted_iota(jnp.int32, (32, B), 1)
    amat[...] = jnp.where(row == col, 1.0, 0.0).astype(F32)
    for j in range(SLOTS):
        each_slot(j, lambda j=j: load(j).wait())

    pl.semaphore_wait(barrier, NS - 1 + NQ - 1)

    def halo_copies(s, j):
        to_right = pltpu.make_async_remote_copy(
            src_ref=raw.at[s, j], dst_ref=halo_l.at[s, j],
            send_sem=hsend.at[s, 0, j], recv_sem=hrecv.at[s, 0, j],
            device_id=(g, right), device_id_type=MESH,
        )
        to_left = pltpu.make_async_remote_copy(
            src_ref=raw.at[s, j], dst_ref=halo_r.at[s, j],
            send_sem=hsend.at[s, 1, j], recv_sem=hrecv.at[s, 1, j],
            device_id=(g, left), device_id_type=MESH,
        )
        return to_right, to_left

    def trans_copy(src, s, sem, other):
        return pltpu.make_async_remote_copy(
            src_ref=src, dst_ref=tall.at[s], send_sem=sem, recv_sem=trecv.at[s],
            device_id=(other, q), device_id_type=MESH,
        )

    def mix_copy(i):
        return pltpu.make_async_remote_copy(
            src_ref=own_mix, dst_ref=mixall.at[g], send_sem=msend.at[i], recv_sem=mrecv.at[g],
            device_id=(lax.rem(g + i, NS), q), device_id_type=MESH,
        )

    def sends_trans(i):
        near = jnp.logical_or(lax.rem(i, 2) == 0, g + i == g + 1 - 2 * core)
        return near

    def each_trans(act):
        @pl.when(g == 0)
        def _():
            for i in range(1, NS):
                act(trans_copy(trans, 0, tsend.at[i], i))

        @pl.when(jnp.logical_and(g > 0, g < STEPS))
        def _():
            act(trans_copy(trans, g, tsend.at[0], g + 1 - 2 * core))
            for i in range(1, 4):
                act(trans_copy(trans, g, tsend.at[i], lax.rem(g + 2 * i, NS)))

    each_trans(lambda c: c.start())
    for j in range(SLOTS):
        def body(j=j):
            for c in halo_copies(0, j):
                c.start()
        each_slot(j, body)

    @pl.when(g < STEPS)
    def _():
        for i in range(1, NS):
            mix_copy(i).start()

    def deliver(s, j):
        return pltpu.make_async_remote_copy(
            src_ref=raw.at[s, j], dst_ref=recv.at[first + j],
            send_sem=deliver_sem.at[s, j], recv_sem=recv_sem.at[first + j],
            device_id=(s, q), device_id_type=MESH,
        )

    def deliver_local(s, j):
        return pltpu.make_async_copy(raw.at[s, j], recv.at[first + j], recv_sem.at[first + j])

    def forwards(s):
        return jnp.logical_and(
            jnp.logical_and(core == lax.rem(s, 2), y != s // 2), jnp.logical_and(s >= 1, s < STEPS)
        )

    def forward(s):
        return trans_copy(tall.at[s], s, fsend.at[s], g + 1 - 2 * core)

    def wait_trans(s):
        pltpu.make_async_copy(tall.at[s], tall.at[s], trecv.at[s]).wait()

    def step(s, carry):
        @pl.when(jnp.logical_and(g != s, jnp.logical_not(forwards(s))))
        def _():
            wait_trans(s)

        @pl.when(forwards(s + 1))
        def _():
            wait_trans(s + 1)
            forward(s + 1).start()

        for d in range(3):
            t = tall[s, d * B:(d + 1) * B, :].T
            if d == 0:
                t = jnp.where(q > 0, t, jnp.zeros_like(t))
            if d == 2:
                t = jnp.where(q < NQ - 1, t, jnp.zeros_like(t))
            tt[d] = t

        for j in range(SLOTS):
            def body(j=j):
                for c in halo_copies(s, j):
                    c.wait_recv()
                parts = [halo_l[s, j], raw[s, j], halo_r[s, j]]
                parts = [dot(tt[d], parts[d]).astype(BF16) for d in range(3)]
                out = dot(jnp.concatenate(parts, axis=1), tall[s])
                raw[s + 1, j] = out.astype(BF16)

                @pl.when(s < STEPS - 1)
                def _():
                    for c in halo_copies(s + 1, j):
                        c.start()

                @pl.when(g != s + 1)
                def _():
                    deliver(s + 1, j).start()

                @pl.when(g == s + 1)
                def _():
                    deliver_local(s + 1, j).start()

            each_slot(j, body)

        @pl.when(g != s)
        def _():
            pltpu.make_async_copy(mixall.at[s], mixall.at[s], mrecv.at[s]).wait()

        @pl.when(s < g)
        def _():
            amat[...] = jnp.dot(mixall[s][:, :32], amat[...], precision=lax.Precision.HIGHEST, preferred_element_type=F32)

        return carry

    lax.fori_loop(0, STEPS, step, 0)

    a = amat[...][:, :32].astype(BF16)
    wide = lax.broadcasted_iota(jnp.int32, (KR, 32), 0) // ROWS
    spread = jnp.where(wide == lax.broadcasted_iota(jnp.int32, (KR, 32), 1), 1.0, 0.0).astype(BF16)
    big = dot(spread, a).astype(BF16)
    big = lax.dot_general(big, spread, (((1,), (1,)), ((), ())), preferred_element_type=F32)
    r0 = lax.rem(lax.broadcasted_iota(jnp.int32, (KR, KR), 0), ROWS)
    r1 = lax.rem(lax.broadcasted_iota(jnp.int32, (KR, KR), 1), ROWS)
    big = jnp.where(r0 == r1, big, 0.0).astype(BF16)

    def wait_recv(w, carry):
        pltpu.make_async_copy(recv.at[w], recv.at[w], recv_sem.at[w]).wait()
        return carry

    lax.fori_loop(0, WM, wait_recv, 0)
    for t in range(B // ROWS):
        rows = recv[:, t * ROWS:(t + 1) * ROWS, :].reshape(KR, B)
        envm[:, t * ROWS:(t + 1) * ROWS, :] = dot(big, rows).astype(BF16).reshape(WM, ROWS, B)
    out_copy = pltpu.make_async_copy(envm, env_out, out_sem)
    out_copy.start()
    renv_copy.wait()

    keep0 = lax.broadcasted_iota(jnp.int32, (B, B), 0) < rank[0]
    keep1 = lax.broadcasted_iota(jnp.int32, (B, B), 1) < rank[0]
    mask = jnp.where(jnp.logical_and(keep0, keep1), 1.0, 0.0).astype(F32)

    def x_copies(k):
        to_right = pltpu.make_async_remote_copy(
            src_ref=xsend.at[k], dst_ref=xl.at[k], send_sem=xsem.at[k, 0], recv_sem=xrecv.at[k, 0],
            device_id=(g, right), device_id_type=MESH,
        )
        to_left = pltpu.make_async_remote_copy(
            src_ref=xsend.at[k], dst_ref=xr.at[k], send_sem=xsem.at[k, 1], recv_sem=xrecv.at[k, 1],
            device_id=(g, left), device_id_type=MESH,
        )
        return to_right, to_left

    def sum_copy(k, i):
        return pltpu.make_async_remote_copy(
            src_ref=psend.at[k], dst_ref=pall.at[k, q], send_sem=psem.at[k], recv_sem=precv.at[k],
            device_id=(g, lax.rem(q + i, NQ)), device_id_type=MESH,
        )

    def start_sum(k, part):
        psend[k] = part
        pall[k, q] = part

        def body(i, carry):
            sum_copy(k, i).start()
            return carry

        lax.fori_loop(1, NQ, body, 0)

    def finish_sum(k):
        others = pall.at[k, pl.ds(0, NQ - 1)]
        pltpu.make_async_copy(others, others, precv.at[k]).wait()
        total = jnp.sum(jnp.sum(pall[k], axis=0), axis=1, keepdims=True)
        return lax.rsqrt(total / (NQ * B * B) + 1e-06)

    cur = start[...] * mask
    part = None
    for k in range(ITERS):
        xsend[k] = cur.astype(BF16)
        for c in x_copies(k):
            c.start()
        if k > 0:
            start_sum(k - 1, part)
            own = jnp.sum(part, axis=1, keepdims=True) / (B * B)
            sigma = lax.rsqrt(jnp.maximum(own, 1e-30))
            x = (cur * sigma).astype(BF16)
        else:
            x = cur.astype(BF16)
        zero = jnp.zeros_like(x)
        xx = jnp.concatenate([jnp.concatenate([x, zero], axis=1), jnp.concatenate([zero, x], axis=1)], axis=0)
        acc = None
        for p in range(PAIRS):
            pair = jnp.concatenate([envm[2 * p], envm[2 * p + 1]], axis=1)
            term = dot(dot(pair, xx).astype(BF16), renv[2 * p:2 * p + 2].reshape(2 * B, B))
            acc = term if acc is None else acc + term
        for c in x_copies(k):
            c.wait_recv()
        near_l = jnp.where(q > 0, xl[k].astype(F32), 0.0)
        near_r = jnp.where(q < NQ - 1, xr[k].astype(F32), 0.0)
        hop = 0.5 * (near_l + near_r)
        if k > 0:
            inv = finish_sum(k - 1)
            cur = mask * (acc * (inv / sigma) + hop * inv)
        else:
            cur = mask * (acc + hop)
        part = jnp.sum(cur * cur, axis=0, keepdims=True)
    start_sum(ITERS - 1, part)

    def drain(s, carry):
        for j in range(SLOTS):
            def body(j=j):
                for c in halo_copies(s, j):
                    c.wait_send()

                @pl.when(g != s + 1)
                def _():
                    deliver(s + 1, j).wait_send()

            each_slot(j, body)

        @pl.when(forwards(s))
        def _():
            forward(s).wait_send()

        return carry

    lax.fori_loop(0, STEPS, drain, 0)
    each_trans(lambda c: c.wait_send())

    @pl.when(g < STEPS)
    def _():
        for i in range(1, NS):
            mix_copy(i).wait_send()

    for k in range(ITERS):
        for c in x_copies(k):
            c.wait_send()
        others = pall.at[k, pl.ds(0, NQ - 1)]
        pltpu.make_async_copy(others, others, psem.at[k]).wait()
    out_copy.wait()
    state[...] = cur * finish_sum(ITERS - 1)


def per_device(env_left, transfer, mpo_mix, right_env, start_state, block_rank):
    dma = pltpu.SemaphoreType.DMA
    vmem = pl.BlockSpec(memory_space=pltpu.VMEM)
    anym = pl.BlockSpec(memory_space=pl.ANY)
    state, env = pl.pallas_call(
        kernel,
        out_shape=(
            jax.ShapeDtypeStruct((B, B), F32),
            jax.ShapeDtypeStruct((WM, B, B), BF16),
        ),
        in_specs=[anym, vmem, vmem, anym, vmem, pl.BlockSpec(memory_space=pltpu.SMEM)],
        out_specs=(vmem, anym),
        scratch_shapes=[
            pltpu.VMEM((NS, SLOTS, B, B), BF16),
            pltpu.VMEM((STEPS, SLOTS, B, B), BF16),
            pltpu.VMEM((STEPS, SLOTS, B, B), BF16),
            pltpu.VMEM((WM, B, B), BF16),
            pltpu.VMEM((WM, B, B), BF16),
            pltpu.VMEM((WM, B, B), BF16),
            pltpu.VMEM((NS, 3 * B, B), BF16),
            pltpu.VMEM((3, B, B), BF16),
            pltpu.VMEM((NS, 32, B), F32),
            pltpu.VMEM((32, B), F32),
            pltpu.VMEM((32, B), F32),
            pltpu.VMEM((ITERS, B, B), BF16),
            pltpu.VMEM((ITERS, B, B), BF16),
            pltpu.VMEM((ITERS, B, B), BF16),
            pltpu.VMEM((ITERS, 1, B), F32),
            pltpu.VMEM((ITERS, NQ, 1, B), F32),
            dma((SLOTS,)),
            dma,
            dma,
            dma((WM,)),
            dma((NS, SLOTS)),
            dma,
            dma((STEPS, 2, SLOTS)),
            dma((STEPS, 2, SLOTS)),
            dma((NS,)),
            dma((NS,)),
            dma((NS,)),
            dma((NS,)),
            dma((NS,)),
            dma((ITERS, 2)),
            dma((ITERS, 2)),
            dma((ITERS,)),
            dma((ITERS,)),
        ],
        compiler_params=pltpu.CompilerParams(
            collective_id=0, has_side_effects=True, vmem_limit_bytes=40 * 1024 * 1024
        ),
    )(
        env_left.reshape(WM, B, B),
        transfer.reshape(3 * B, B),
        mpo_mix.reshape(WM, WM),
        right_env.reshape(WM, B, B),
        start_state.reshape(B, B),
        block_rank,
    )
    return state.reshape(1, 1, B, B), env.reshape(1, WM, 1, B, B)


def solution(mesh):
    in_specs = (
        P(None, "blk", None, None),
        P("sec", "blk", None, None, None),
        P("sec", None, None),
        P("sec", None, "blk", None, None),
        P("sec", "blk", None, None),
        P("blk"),
    )
    out_specs = (P("sec", "blk", None, None), P("sec", None, "blk", None, None))
    return jax.shard_map(
        per_device, mesh=mesh, in_specs=in_specs, out_specs=out_specs, check_vma=False
    )
```

time: 707 us -> 88.2 us (0.12)
  the two profiles are of different devices: /device:TPU:136 before, /device:TPU:16 now
where the time goes in v1:
time: 88.2 us; the launch traced here: 87.9 us
  Pallas kernels  80.3 us (91%)
  local copies, waits for them, and re-layouts  6.29 us (7%)
  between operations  1.29 us (1%)
    pallas_call x1, Pallas kernels, per_device(): pl.pallas_call(kernel, out_shape=(jax.ShapeDtypeStruct((B, B), F32), jax....  80.3 us
    unnamed x11, local copies, waits for them, and re-layouts  6.29 us

profile of v1, /device:TPU:16, one launch (start us, length us, event | category | flops | bytes accessed | tf_op | source)
XLA Modules:
  0.0 87.9 jit_solution(18166015386783180552)
XLA Ops:
  1.3 0.7 copy.11
  2.0 0.0 copy-start
  2.0 1.2 %copy-done = bf16[26,1,128,128]{3,2,1,0:T(8,128)(2,1)S(1)} copy-done((bf16[26,1,128,128]{3,2,1,0:T(8,128)(2,1)S(1)}, bf16[26,1,128,128]{3,2,1,0:T(8,128)(2,1)}, u32[]{:S(2)}) %copy-start) | copy-done | bytes 851992
  3.1 0.0 copy-start.1
  3.1 1.2 %copy-done.1 = bf16[1,26,1,128,128]{4,3,2,1,0:T(8,128)(2,1)S(1)} copy-done((bf16[1,26,1,128,128]{4,3,2,1,0:T(8,128)(2,1)S(1)}, bf16[1,26,1,128,128]{4,3,2,1,0:T(8,128)(2,1)}, u32[]{:S(2)}) %copy-start.1) | copy-done | bytes 851992
  4.3 0.0 copy-start.2
  4.3 0.9 %copy-done.2 = bf16[1,1,3,128,128]{4,3,2,1,0:T(8,128)(2,1)S(1)} copy-done((bf16[1,1,3,128,128]{4,3,2,1,0:T(8,128)(2,1)S(1)}, bf16[1,1,3,128,128]{4,3,2,1,0:T(8,128)(2,1)}, u32[]{:S(2)}) %copy-start.2) | copy-done | bytes 98328
  5.2 0.0 copy-start.3
  5.2 0.8 copy-done.3
  6.0 80.3 %shard_map.77 = (f32[128,128]{1,0:T(8,128)S(1)}, bf16[26,128,128]{2,1,0:T(8,128)(2,1)S(1)}) custom-call(bf16[26,128,128]{2,1,0:T(8,128)(2,1)S(1)} %bitcast.11, bf16[384,128]{1,0:T(8,128)(2,1)S(1)} %bitcast.14, f32[26,26]{1,0:T(8,128)S(1)} %bitcast.15, bf16[26,128,128]{2,1,0:T(8,128)(2,1)S(1)} %bitcast.12, f32[128,128]{1,0:T(8,128)S(1)} %bitcast.16, ...), custom_call_target="tpu_custom_call" | custom-call | tf_op jit(solution)/shard_map/pallas_call | solution.py:350
  86.4 0.6 copy.15
  87.0 0.9 %copy.16 = bf16[1,26,1,128,128]{4,3,2,1,0:T(8,128)(2,1)} copy(bf16[1,26,1,128,128]{4,3,2,1,0:T(8,128)(2,1)S(1)} %bitcast.13) | data formatting | bytes 1703936
Async XLA Ops:
  2.0 1.2 %copy-start = (bf16[26,1,128,128]{3,2,1,0:T(8,128)(2,1)S(1)}, bf16[26,1,128,128]{3,2,1,0:T(8,128)(2,1)}, u32[]{:S(2)}) copy-start(bf16[26,1,128,128]{3,2,1,0:T(8,128)(2,1)} %param.6) | copy-start | bytes 2555908
  3.1 1.2 %copy-start.1 = (bf16[1,26,1,128,128]{4,3,2,1,0:T(8,128)(2,1)S(1)}, bf16[1,26,1,128,128]{4,3,2,1,0:T(8,128)(2,1)}, u32[]{:S(2)}) copy-start(bf16[1,26,1,128,128]{4,3,2,1,0:T(8,128)(2,1)} %param.9) | copy-start | bytes 2555908
  4.3 0.9 %copy-start.2 = (bf16[1,1,3,128,128]{4,3,2,1,0:T(8,128)(2,1)S(1)}, bf16[1,1,3,128,128]{4,3,2,1,0:T(8,128)(2,1)}, u32[]{:S(2)}) copy-start(bf16[1,1,3,128,128]{4,3,2,1,0:T(8,128)(2,1)} %param.7) | copy-start | bytes 294916
  5.2 0.8 copy-start.3

commit v2 on v1

v2 whole, which is shorter than its diff:
```python
import jax
import jax.numpy as jnp
from jax import lax
from jax.experimental import pallas as pl
from jax.experimental.pallas import tpu as pltpu
from jax.sharding import PartitionSpec as P

ITERS = 4
B = 128
WM = 26
NS = 8
NQ = 32
SLOTS = 4
STEPS = NS - 1
PAIRS = WM // 2
ROWS = 16
KR = WM * ROWS
FIRSTS = (0, 4, 7, 11, 14, 17, 20, 23)
ORDER = [f + j for j in range(3) for f in FIRSTS] + [3, 10]
GROUPS = (range(0, 4), range(4, 8), range(8, 13))
AUX = 16
MSG = B + AUX
SENDS = ((0, 1), (0, -1), (1, 1), (1, -1), (1, 2), (1, -2), (2, 1), (2, -1), (3, 1), (3, -1))
LOG_EPS = -19.931568569324174
LOG_N = 19.0
MESH = pl.DeviceIdType.MESH
F32 = jnp.float32
BF16 = jnp.bfloat16


def dot(a, b):
    return jnp.dot(a, b, preferred_element_type=F32)


def kernel(
    env_hbm, trans_hbm, mix_hbm, renv_hbm, start_hbm, rank, state, env_out,
    raw, halo_l, halo_r, recv, renv, renvp, tall, tt, mixall, amat, mix_in, own_mix,
    start, outbox, inbox, psend, pall,
    load_sem, in_sem, recv_sem, deliver_sem,
    hrecv, hsend, trecv, tsend, fsend, mrecv, msend,
    xrecv, xsem, precv, psem,
):
    g = lax.axis_index("sec")
    q = lax.axis_index("blk")
    y = g // 2
    core = lax.rem(g, 2)
    right = lax.rem(q + 1, NQ)
    left = lax.rem(q + NQ - 1, NQ)
    first = 3 * g + jnp.where(g >= 1, 1, 0) + jnp.where(g >= 3, 1, 0)
    four = jnp.logical_or(g == 0, g == 2)

    loads = [
        pltpu.make_async_copy(trans_hbm, tall.at[g], in_sem.at[0]),
        pltpu.make_async_copy(mix_hbm, mix_in, in_sem.at[1]),
        pltpu.make_async_copy(start_hbm, start, in_sem.at[2]),
        pltpu.make_async_copy(renv_hbm, renv, in_sem.at[3]),
    ]

    def each_slot(j, body):
        if j < SLOTS - 1:
            body()
        else:
            pl.when(four)(body)

    def load(j):
        return pltpu.make_async_copy(env_hbm.at[first + j], raw.at[0, j], load_sem.at[j])

    loads[0].start()
    for j in range(SLOTS):
        each_slot(j, lambda j=j: load(j).start())
    for c in loads[1:]:
        c.start()

    barrier = pltpu.get_barrier_semaphore()

    def greet_sec(i, carry):
        pl.semaphore_signal(barrier, inc=1, device_id=(lax.rem(g + i, NS), q), device_id_type=MESH)
        return carry

    def greet_blk(i, carry):
        pl.semaphore_signal(barrier, inc=1, device_id=(g, lax.rem(q + i, NQ)), device_id_type=MESH)
        return carry

    lax.fori_loop(1, NS, greet_sec, 0)
    lax.fori_loop(1, NQ, greet_blk, 0)

    @pl.when(g == 0)
    def _():
        def body(w, carry):
            pltpu.make_async_copy(env_hbm.at[w], recv.at[w], recv_sem.at[w]).start()
            return carry

        lax.fori_loop(0, WM, body, 0)

    own_mix[...] = jnp.zeros_like(own_mix)
    loads[1].wait()
    own_mix[:WM, :WM] = mix_in[...].reshape(WM, WM)
    mixall[g] = own_mix[...]
    row = lax.broadcasted_iota(jnp.int32, (32, B), 0)
    col = lax.broadcasted_iota(jnp.int32, (32, B), 1)
    amat[...] = jnp.where(row == col, 1.0, 0.0).astype(F32)
    keep0 = lax.broadcasted_iota(jnp.int32, (B, B), 0)
    keep1 = lax.broadcasted_iota(jnp.int32, (B, B), 1)
    larger = jnp.maximum(keep0, keep1).astype(F32)
    my_rank = rank[0].astype(F32)
    mask = jnp.where(larger < my_rank, 1.0, 0.0).astype(F32)
    loads[2].wait()
    outbox[0, :B, :] = (start[...] * mask).astype(BF16)
    outbox[0, B:, :] = jnp.full((AUX, B), my_rank, F32).astype(BF16)
    loads[0].wait()
    for j in range(SLOTS):
        each_slot(j, lambda j=j: load(j).wait())

    pl.semaphore_wait(barrier, NS - 1 + NQ - 1)

    def halo_copies(s, j):
        to_right = pltpu.make_async_remote_copy(
            src_ref=raw.at[s, j], dst_ref=halo_l.at[s, j],
            send_sem=hsend.at[s, 0, j], recv_sem=hrecv.at[s, 0, j],
            device_id=(g, right), device_id_type=MESH,
        )
        to_left = pltpu.make_async_remote_copy(
            src_ref=raw.at[s, j], dst_ref=halo_r.at[s, j],
            send_sem=hsend.at[s, 1, j], recv_sem=hrecv.at[s, 1, j],
            device_id=(g, left), device_id_type=MESH,
        )
        return to_right, to_left

    def trans_copy(src, s, sem, other):
        return pltpu.make_async_remote_copy(
            src_ref=src, dst_ref=tall.at[s], send_sem=sem, recv_sem=trecv.at[s],
            device_id=(other, q), device_id_type=MESH,
        )

    def mix_copy(i):
        return pltpu.make_async_remote_copy(
            src_ref=own_mix, dst_ref=mixall.at[g], send_sem=msend.at[i], recv_sem=mrecv.at[g],
            device_id=(lax.rem(g + i, NS), q), device_id_type=MESH,
        )

    def each_trans(act):
        @pl.when(g == 0)
        def _():
            for i in range(1, NS):
                act(trans_copy(tall.at[g], 0, tsend.at[i], i))

        @pl.when(jnp.logical_and(g > 0, g < STEPS))
        def _():
            act(trans_copy(tall.at[g], g, tsend.at[0], g + 1 - 2 * core))
            for i in range(1, 4):
                act(trans_copy(tall.at[g], g, tsend.at[i], lax.rem(g + 2 * i, NS)))

    each_trans(lambda c: c.start())
    for j in range(SLOTS):
        def body(j=j):
            for c in halo_copies(0, j):
                c.start()
        each_slot(j, body)

    @pl.when(g < STEPS)
    def _():
        for i in range(1, NS):
            mix_copy(i).start()

    def box_copy(i):
        m, far = SENDS[i]
        return pltpu.make_async_remote_copy(
            src_ref=outbox.at[m], dst_ref=inbox.at[i], send_sem=xsem.at[i], recv_sem=xrecv.at[i],
            device_id=(g, lax.rem(q + (NQ + far), NQ)), device_id_type=MESH,
        )

    def send(m):
        for i in range(len(SENDS)):
            if SENDS[i][0] == m:
                box_copy(i).start()

    send(0)

    def deliver(s, j):
        return pltpu.make_async_remote_copy(
            src_ref=raw.at[s, j], dst_ref=recv.at[first + j],
            send_sem=deliver_sem.at[s, j], recv_sem=recv_sem.at[first + j],
            device_id=(s, q), device_id_type=MESH,
        )

    def deliver_local(s, j):
        return pltpu.make_async_copy(raw.at[s, j], recv.at[first + j], recv_sem.at[first + j])

    def forwards(s):
        return jnp.logical_and(
            jnp.logical_and(core == lax.rem(s, 2), y != s // 2), jnp.logical_and(s >= 1, s < STEPS)
        )

    def forward(s):
        return trans_copy(tall.at[s], s, fsend.at[s], g + 1 - 2 * core)

    def wait_trans(s):
        pltpu.make_async_copy(tall.at[s], tall.at[s], trecv.at[s]).wait()

    def step(s, carry):
        @pl.when(jnp.logical_and(g != s, jnp.logical_not(forwards(s))))
        def _():
            wait_trans(s)

        @pl.when(forwards(s + 1))
        def _():
            wait_trans(s + 1)
            forward(s + 1).start()

        for d in range(3):
            t = tall[s, d * B:(d + 1) * B, :].T
            if d == 0:
                t = jnp.where(q > 0, t, jnp.zeros_like(t))
            if d == 2:
                t = jnp.where(q < NQ - 1, t, jnp.zeros_like(t))
            tt[d] = t

        for j in range(SLOTS):
            def body(j=j):
                for c in halo_copies(s, j):
                    c.wait_recv()
                parts = [halo_l[s, j], raw[s, j], halo_r[s, j]]
                parts = [dot(tt[d], parts[d]).astype(BF16) for d in range(3)]
                out = dot(jnp.concatenate(parts, axis=1), tall[s])
                raw[s + 1, j] = out.astype(BF16)

                @pl.when(s < STEPS - 1)
                def _():
                    for c in halo_copies(s + 1, j):
                        c.start()

                @pl.when(g != s + 1)
                def _():
                    deliver(s + 1, j).start()

                @pl.when(g == s + 1)
                def _():
                    deliver_local(s + 1, j).start()

            each_slot(j, body)

        @pl.when(g != s)
        def _():
            pltpu.make_async_copy(mixall.at[s], mixall.at[s], mrecv.at[s]).wait()

        @pl.when(s < g)
        def _():
            amat[...] = jnp.dot(mixall[s][:, :32], amat[...], precision=lax.Precision.HIGHEST, preferred_element_type=F32)

        return carry

    lax.fori_loop(0, STEPS, step, 0)

    a = amat[...][:, :32].astype(BF16)
    wide = lax.broadcasted_iota(jnp.int32, (KR, 32), 0) // ROWS
    spread = jnp.where(wide == lax.broadcasted_iota(jnp.int32, (KR, 32), 1), 1.0, 0.0).astype(BF16)
    r0 = lax.rem(lax.broadcasted_iota(jnp.int32, (KR, KR), 0), ROWS)
    r1 = lax.rem(lax.broadcasted_iota(jnp.int32, (KR, KR), 1), ROWS)

    def widen(half):
        full = lax.dot_general(half.astype(BF16), spread, (((1,), (1,)), ((), ())), preferred_element_type=F32)
        return jnp.where(r0 == r1, full, 0.0).astype(BF16)

    turned = widen(lax.dot_general(spread, a, (((1,), (1,)), ((), ())), preferred_element_type=F32))
    loads[3].wait()
    for t in range(B // ROWS):
        rows = renv[:, t * ROWS:(t + 1) * ROWS, :].reshape(KR, B)
        mixed = dot(turned, rows).astype(BF16).reshape(WM, ROWS, B)
        for i, w in enumerate(ORDER):
            at = (i % 2) * B + t * ROWS
            renvp[i // 2, at:at + ROWS, :] = mixed[w]
    big = widen(dot(spread, a))

    def pairs(xx, group):
        acc = None
        for p in group:
            pair = jnp.concatenate([recv[ORDER[2 * p]], recv[ORDER[2 * p + 1]]], axis=1)
            term = dot(dot(pair, xx).astype(BF16), renvp[p])
            acc = term if acc is None else acc + term
        return acc

    def twice(x):
        zero = jnp.zeros_like(x)
        return jnp.concatenate([jnp.concatenate([x, zero], axis=1), jnp.concatenate([zero, x], axis=1)], axis=0)

    def apply(x):
        return pairs(twice(x), range(PAIRS)) * mask

    def largest(v):
        return jnp.max(jnp.max(jnp.abs(v), axis=0, keepdims=True), axis=1, keepdims=True)

    def total(v):
        return jnp.sum(jnp.sum(v, axis=0, keepdims=True), axis=1, keepdims=True)

    def log2(v):
        return jnp.log(jnp.maximum(v, 1e-30)) * 1.4426950408889634

    def norm(v, e):
        up = 2.0 * jnp.floor(0.5 * log2(largest(v)) + 0.5)
        return v * jnp.exp2(-up), e + up

    def add(terms):
        top = terms[0][1]
        for _, e in terms[1:]:
            top = jnp.maximum(top, e)
        value = None
        for m, e in terms:
            part = m * jnp.exp2(e - top)
            value = part if value is None else value + part
        return value, top

    def post(m, value, e):
        outbox[m, :B, :] = value
        outbox[m, B:, :] = jnp.broadcast_to(0.5 * e, (AUX, B)).astype(BF16)
        send(m)

    def take(m, far):
        i = SENDS.index((m, far))
        box_copy(i).wait_recv()
        there = jnp.logical_and(q - far >= 0, q - far < NQ)
        value = jnp.where(there, inbox[i, :B, :].astype(F32), 0.0)
        return value, inbox[i, B:, :].astype(F32)[:1, :1]

    def take_scaled(m, far):
        value, e = take(m, far)
        return value, 2.0 * e

    def size(m, e):
        return log2(total(m * m)) + 2.0 * e

    x = outbox[0, :B, :]
    xx = twice(x)
    start_l, rank_l = take(0, 1)
    start_r, rank_r = take(0, -1)
    hop = 0.5 * (start_l + start_r)
    acc = None
    for group in GROUPS:
        for p in group:
            for w in ORDER[2 * p:2 * p + 2]:
                pltpu.make_async_copy(recv.at[w], recv.at[w], recv_sem.at[w]).wait()
        part = pairs(xx, group)
        acc = part if acc is None else acc + part
    m1, l1 = norm(mask * (acc + hop), jnp.zeros((1, 1), F32))
    x1 = m1.astype(BF16)
    post(1, x1, l1)
    mp, lp = norm(apply(x1), l1)
    post(2, mp.astype(BF16), lp)
    sizes = [size(m1, l1)]
    half = 0.5 * mask
    half_l = jnp.where(larger < rank_l, 0.5, 0.0).astype(F32)
    half_r = jnp.where(larger < rank_r, 0.5, 0.0).astype(F32)
    m1_l, l1_l = take_scaled(1, 1)
    m1_r, l1_r = take_scaled(1, -1)
    m2, l2 = norm(*add([(mp, lp), (half * m1_l, l1_l), (half * m1_r, l1_r)]))
    r, lr = norm(apply(m2.astype(BF16)), l2)
    sizes.append(size(m2, l2))
    m1_ll, l1_ll = take_scaled(1, 2)
    m1_rr, l1_rr = take_scaled(1, -2)
    mp_l, lp_l = take_scaled(2, 1)
    mp_r, lp_r = take_scaled(2, -1)
    m2_l, l2_l = add([(mp_l, lp_l), (half_l * m1, l1), (half_l * m1_ll, l1_ll)])
    m2_r, l2_r = add([(mp_r, lp_r), (half_r * m1, l1), (half_r * m1_rr, l1_rr)])
    m2_l = jnp.where(q > 0, m2_l, 0.0)
    m2_r = jnp.where(q < NQ - 1, m2_r, 0.0)
    m3, l3 = norm(*add([(r, lr), (half * m2_l, l2_l), (half * m2_r, l2_r)]))
    x3 = m3.astype(BF16)
    post(3, x3, l3)
    v, lv = norm(apply(x3), l3)
    sizes.append(size(m3, l3))
    for t in range(B // ROWS):
        rows = recv[:, t * ROWS:(t + 1) * ROWS, :].reshape(KR, B)
        env_out[:, t * ROWS:(t + 1) * ROWS, :] = dot(big, rows).astype(BF16).reshape(WM, ROWS, B)
    m3_l, l3_l = take_scaled(3, 1)
    m3_r, l3_r = take_scaled(3, -1)
    m4, l4 = norm(*add([(v, lv), (half * m3_l, l3_l), (half * m3_r, l3_r)]))
    sizes.append(size(m4, l4))

    lane = lax.broadcasted_iota(jnp.int32, (1, B), 1)
    line = jnp.full((1, B), -1e30, F32)
    for k in range(ITERS):
        line = jnp.where(lane == k, sizes[k] + ((ITERS - 1 - k) * LOG_EPS - LOG_N), line)
    psend[...] = line
    pall[q] = line

    def sum_copy(i):
        return pltpu.make_async_remote_copy(
            src_ref=psend, dst_ref=pall.at[q], send_sem=psem, recv_sem=precv,
            device_id=(g, lax.rem(q + i, NQ)), device_id_type=MESH,
        )

    def start_sum(i, carry):
        sum_copy(i).start()
        return carry

    lax.fori_loop(1, NQ, start_sum, 0)

    def drain(s, carry):
        for j in range(SLOTS):
            def body(j=j):
                for c in halo_copies(s, j):
                    c.wait_send()

                @pl.when(g != s + 1)
                def _():
                    deliver(s + 1, j).wait_send()

            each_slot(j, body)

        @pl.when(forwards(s))
        def _():
            forward(s).wait_send()

        return carry

    lax.fori_loop(0, STEPS, drain, 0)
    each_trans(lambda c: c.wait_send())

    @pl.when(g < STEPS)
    def _():
        for i in range(1, NS):
            mix_copy(i).wait_send()

    for i in range(len(SENDS)):
        box_copy(i).wait_send()
    others = pall.at[pl.ds(0, NQ - 1)]
    pltpu.make_async_copy(others, others, psem).wait()
    pltpu.make_async_copy(others, others, precv).wait()
    logs = pall[...].reshape(NQ, B)
    top = jnp.max(jnp.max(logs, axis=0, keepdims=True), axis=1, keepdims=True)
    top = jnp.maximum(top, ITERS * LOG_EPS)
    square = total(jnp.exp2(logs - top)) + jnp.exp2(ITERS * LOG_EPS - top)
    state[...] = m4 * (jnp.exp2(l4 - 0.5 * top) * lax.rsqrt(square))


def per_device(env_left, transfer, mpo_mix, right_env, start_state, block_rank):
    dma = pltpu.SemaphoreType.DMA
    vmem = pl.BlockSpec(memory_space=pltpu.VMEM)
    hbm = pl.BlockSpec(memory_space=pltpu.HBM)
    state, env = pl.pallas_call(
        kernel,
        out_shape=(
            jax.ShapeDtypeStruct((B, B), F32),
            jax.ShapeDtypeStruct((WM, B, B), BF16),
        ),
        in_specs=[hbm, hbm, hbm, hbm, hbm, pl.BlockSpec(memory_space=pltpu.SMEM)],
        out_specs=(vmem, vmem),
        scratch_shapes=[
            pltpu.VMEM((NS, SLOTS, B, B), BF16),
            pltpu.VMEM((STEPS, SLOTS, B, B), BF16),
            pltpu.VMEM((STEPS, SLOTS, B, B), BF16),
            pltpu.VMEM((WM, B, B), BF16),
            pltpu.VMEM((WM, B, B), BF16),
            pltpu.VMEM((PAIRS, 2 * B, B), BF16),
            pltpu.VMEM((NS, 3 * B, B), BF16),
            pltpu.VMEM((3, B, B), BF16),
            pltpu.VMEM((NS, 32, B), F32),
            pltpu.VMEM((32, B), F32),
            pltpu.VMEM((WM, 1, WM), F32),
            pltpu.VMEM((32, B), F32),
            pltpu.VMEM((B, B), F32),
            pltpu.VMEM((4, MSG, B), BF16),
            pltpu.VMEM((len(SENDS), MSG, B), BF16),
            pltpu.VMEM((1, B), F32),
            pltpu.VMEM((NQ, 1, B), F32),
            dma((SLOTS,)),
            dma((4,)),
            dma((WM,)),
            dma((NS, SLOTS)),
            dma((STEPS, 2, SLOTS)),
            dma((STEPS, 2, SLOTS)),
            dma((NS,)),
            dma((NS,)),
            dma((NS,)),
            dma((NS,)),
            dma((NS,)),
            dma((len(SENDS),)),
            dma((len(SENDS),)),
            dma,
            dma,
        ],
        compiler_params=pltpu.CompilerParams(
            collective_id=0, has_side_effects=True, vmem_limit_bytes=40 * 1024 * 1024
        ),
    )(
        *(
            pltpu.with_memory_space_constraint(value, pltpu.HBM)
            for value in (
                env_left.reshape(WM, B, B),
                transfer.reshape(3 * B, B),
                jnp.transpose(mpo_mix, (1, 0, 2)),
                right_env.reshape(WM, B, B),
                start_state.reshape(B, B),
            )
        ),
        block_rank,
    )
    return state.reshape(1, 1, B, B), env.reshape(1, WM, 1, B, B)


def solution(mesh):
    in_specs = (
        P(None, "blk", None, None),
        P("sec", "blk", None, None, None),
        P("sec", None, None),
        P("sec", None, "blk", None, None),
        P("sec", "blk", None, None),
        P("blk"),
    )
    out_specs = (P("sec", "blk", None, None), P("sec", None, "blk", None, None))
    return jax.shard_map(
        per_device, mesh=mesh, in_specs=in_specs, out_specs=out_specs, check_vma=False
    )
```

time: 88.2 us -> 72.3 us (0.82)
  the two profiles are of different devices: /device:TPU:16 before, /device:TPU:24 now
where the time goes in v2:
time: 72.3 us; the launch traced here: 71.6 us
  Pallas kernels  68.7 us (95%)
  local copies, waits for them, and re-layouts  1.53 us (2%)
  between operations  1.29 us (2%)
    pallas_call x1, Pallas kernels, per_device(): pl.pallas_call(kernel, out_shape=(jax.ShapeDtypeStruct((B, B), F32), jax....  68.7 us
    unnamed x2, local copies, waits for them, and re-layouts  1.53 us

profile of v2, /device:TPU:24, one launch (start us, length us, event | category | flops | bytes accessed | tf_op | source)
XLA Modules:
  0.0 71.6 jit_solution(2062641868820552609)
XLA Ops:
  1.3 68.7 %shard_map.77 = (f32[128,128]{1,0:T(8,128)S(1)}, bf16[26,128,128]{2,1,0:T(8,128)(2,1)S(1)}) custom-call(bf16[26,128,128]{2,1,0:T(8,128)(2,1)} %bitcast.11, bf16[384,128]{1,0:T(8,128)(2,1)} %bitcast.13, f32[26,1,26]{2,1,0:T(1,128)} %bitcast.15, bf16[26,128,128]{2,1,0:T(8,128)(2,1)} %bitcast.12, f32[128,128]{1,0:T(8,128)} %bitcast.14, s32[1]{0:T(128)S(6)} %copy.11.rank), custom_call_target="tpu_custom_call" | custom-call | tf_op jit(solution)/shard_map/pallas_call | solution.py:439
  70.0 0.6 copy.12
  70.7 0.9 %copy.13 = bf16[1,26,1,128,128]{4,3,2,1,0:T(8,128)(2,1)} copy(bf16[1,26,1,128,128]{4,3,2,1,0:T(8,128)(2,1)S(1)} %bitcast.9) | data formatting | bytes 1703936

commit v3 on v2

--- a/solution.py
+++ b/solution.py
@@ -10,6 +10,7 @@
 WM = 26
 NS = 8
 NQ = 32
+NX = 4
 SLOTS = 4
 STEPS = NS - 1
 PAIRS = WM // 2
@@ -34,10 +35,10 @@
 
 def kernel(
     env_hbm, trans_hbm, mix_hbm, renv_hbm, start_hbm, rank, state, env_out,
-    raw, halo_l, halo_r, recv, renv, renvp, tall, tt, mixall, amat, mix_in, own_mix,
+    raw, halo, halo2, fart, ft, recv, renv, renvp, tall, tt, mixall, amat, mix_in, own_mix,
     start, outbox, inbox, psend, pall,
     load_sem, in_sem, recv_sem, deliver_sem,
-    hrecv, hsend, trecv, tsend, fsend, mrecv, msend,
+    hrecv, hsend, h2recv, h2send, ftrecv, ftsend, trecv, tsend, fsend, mrecv, msend,
     xrecv, xsem, precv, psem,
 ):
     g = lax.axis_index("sec")
@@ -48,6 +49,11 @@
     left = lax.rem(q + NQ - 1, NQ)
     first = 3 * g + jnp.where(g >= 1, 1, 0) + jnp.where(g >= 3, 1, 0)
     four = jnp.logical_or(g == 0, g == 2)
+    x_at = lax.rem(q, NX)
+    far = jnp.logical_or(x_at == 0, x_at == NX - 1)
+    side = jnp.where(x_at == 0, 0, 1)
+    beyond = jnp.where(x_at == 0, left, right)
+    two_off = lax.rem(jnp.where(x_at == 2, q + 2, q + (NQ - 2)), NQ)
 
     loads = [
         pltpu.make_async_copy(trans_hbm, tall.at[g], in_sem.at[0]),
@@ -83,6 +89,11 @@
 
     lax.fori_loop(1, NS, greet_sec, 0)
     lax.fori_loop(1, NQ, greet_blk, 0)
+
+    @pl.when(jnp.logical_and(far, core == 0))
+    def _():
+        pl.semaphore_signal(barrier, inc=1, device_id=(g + 1, beyond), device_id_type=MESH)
+
 
     @pl.when(g == 0)
     def _():
@@ -111,20 +122,57 @@
     for j in range(SLOTS):
         each_slot(j, lambda j=j: load(j).wait())
 
-    pl.semaphore_wait(barrier, NS - 1 + NQ - 1)
-
-    def halo_copies(s, j):
-        to_right = pltpu.make_async_remote_copy(
-            src_ref=raw.at[s, j], dst_ref=halo_l.at[s, j],
-            send_sem=hsend.at[s, 0, j], recv_sem=hrecv.at[s, 0, j],
-            device_id=(g, right), device_id_type=MESH,
-        )
-        to_left = pltpu.make_async_remote_copy(
-            src_ref=raw.at[s, j], dst_ref=halo_r.at[s, j],
-            send_sem=hsend.at[s, 1, j], recv_sem=hrecv.at[s, 1, j],
-            device_id=(g, left), device_id_type=MESH,
-        )
-        return to_right, to_left
+    pl.semaphore_wait(barrier, NS - 1 + NQ - 1 + jnp.where(jnp.logical_and(far, core == 1), 1, 0))
+
+    def crossed(s):
+        return jnp.logical_or(s == 0, lax.rem(s, 2) == 1)
+
+    def halo_copy(s, j, to):
+        return pltpu.make_async_remote_copy(
+            src_ref=raw.at[s, j], dst_ref=halo.at[s, 1 - to, j],
+            send_sem=hsend.at[s, to, j], recv_sem=hrecv.at[s, 1 - to, j],
+            device_id=(g, right if to else left), device_id_type=MESH,
+        )
+
+    def inside(to):
+        return x_at != (NX - 1 if to else 0)
+
+    def each_halo(s, j, act):
+        for to in range(2):
+            pl.when(jnp.logical_or(inside(to), crossed(s)))(lambda to=to: act(halo_copy(s, j, to)))
+
+    def wait_halo(s, j):
+        for at in range(2):
+            @pl.when(jnp.logical_or(inside(at), crossed(s)))
+            def _():
+                halo_copy(s, j, 1 - at).wait_recv()
+
+    def halo2_copy(s, j):
+        return pltpu.make_async_remote_copy(
+            src_ref=raw.at[s, j], dst_ref=halo2.at[s // 2, j],
+            send_sem=h2send.at[s // 2, j], recv_sem=h2recv.at[s // 2, j],
+            device_id=(g, two_off), device_id_type=MESH,
+        )
+
+    def each_halo2(s, j, act):
+        pl.when(jnp.logical_and(jnp.logical_not(far), lax.rem(s, 2) == 1))(lambda: act(halo2_copy(s, j)))
+
+    def start_halo(s, j):
+        each_halo(s, j, lambda c: c.start())
+        each_halo2(s, j, lambda c: c.start())
+
+    def far_trans(s, i):
+        return pltpu.make_async_remote_copy(
+            src_ref=tall.at[s], dst_ref=fart.at[s // 2],
+            send_sem=ftsend.at[s // 2, i], recv_sem=ftrecv.at[s // 2],
+            device_id=(g - i, beyond), device_id_type=MESH,
+        )
+
+    def each_far_trans(s, act):
+        @pl.when(jnp.logical_and(jnp.logical_and(far, core == 1), jnp.logical_and(lax.rem(s, 2) == 1, s < STEPS)))
+        def _():
+            for i in range(2):
+                act(far_trans(s, i))
 
     def trans_copy(src, s, sem, other):
         return pltpu.make_async_remote_copy(
@@ -150,12 +198,9 @@
             for i in range(1, 4):
                 act(trans_copy(tall.at[g], g, tsend.at[i], lax.rem(g + 2 * i, NS)))
 
+    for j in range(SLOTS):
+        each_slot(j, lambda j=j: start_halo(0, j))
     each_trans(lambda c: c.start())
-    for j in range(SLOTS):
-        def body(j=j):
-            for c in halo_copies(0, j):
-                c.start()
-        each_slot(j, body)
 
     @pl.when(g < STEPS)
     def _():
@@ -197,15 +242,23 @@
     def wait_trans(s):
         pltpu.make_async_copy(tall.at[s], tall.at[s], trecv.at[s]).wait()
 
+    def pass_on(s):
+        @pl.when(forwards(s))
+        def _():
+            wait_trans(s)
+            forward(s).start()
+
+        each_far_trans(s, lambda c: c.start())
+
+    pass_on(1)
+
     def step(s, carry):
         @pl.when(jnp.logical_and(g != s, jnp.logical_not(forwards(s))))
         def _():
             wait_trans(s)
 
-        @pl.when(forwards(s + 1))
-        def _():
-            wait_trans(s + 1)
-            forward(s + 1).start()
+        pass_on(s + 2)
+        redo = jnp.logical_and(far, lax.rem(s, 2) == 1)
 
         for d in range(3):
             t = tall[s, d * B:(d + 1) * B, :].T
@@ -215,19 +268,18 @@
                 t = jnp.where(q < NQ - 1, t, jnp.zeros_like(t))
             tt[d] = t
 
+        def carry_on(parts, turned, tensor):
+            parts = [dot(turned[d], parts[d]).astype(BF16) for d in range(3)]
+            return dot(jnp.concatenate(parts, axis=1), tensor).astype(BF16)
+
         for j in range(SLOTS):
             def body(j=j):
-                for c in halo_copies(s, j):
-                    c.wait_recv()
-                parts = [halo_l[s, j], raw[s, j], halo_r[s, j]]
-                parts = [dot(tt[d], parts[d]).astype(BF16) for d in range(3)]
-                out = dot(jnp.concatenate(parts, axis=1), tall[s])
-                raw[s + 1, j] = out.astype(BF16)
+                wait_halo(s, j)
+                raw[s + 1, j] = carry_on([halo[s, 0, j], raw[s, j], halo[s, 1, j]], tt, tall[s])
 
                 @pl.when(s < STEPS - 1)
                 def _():
-                    for c in halo_copies(s + 1, j):
-                        c.start()
+                    start_halo(s + 1, j)
 
                 @pl.when(g != s + 1)
                 def _():
@@ -238,6 +290,21 @@
                     deliver_local(s + 1, j).start()
 
             each_slot(j, body)
+
+        @pl.when(redo)
+        def _():
+            pltpu.make_async_copy(fart.at[s // 2], fart.at[s // 2], ftrecv.at[s // 2]).wait()
+            for d in range(3):
+                ft[d] = fart[s // 2, d * B:(d + 1) * B, :].T
+            for j in range(SLOTS):
+                def again(j=j):
+                    halo2_copy(s, j).wait_recv()
+                    mine, other = raw[s, j], halo2[s // 2, j]
+                    low = jnp.where(x_at == 0, other, mine)
+                    high = jnp.where(x_at == 0, mine, other)
+                    halo[s + 1, side, j] = carry_on([low, halo[s, side, j], high], ft, fart[s // 2])
+
+                each_slot(j, again)
 
         @pl.when(g != s)
         def _():
@@ -397,8 +464,8 @@
     def drain(s, carry):
         for j in range(SLOTS):
             def body(j=j):
-                for c in halo_copies(s, j):
-                    c.wait_send()
+                each_halo(s, j, lambda c: c.wait_send())
+                each_halo2(s, j, lambda c: c.wait_send())
 
                 @pl.when(g != s + 1)
                 def _():
@@ -410,6 +477,7 @@
         def _():
             forward(s).wait_send()
 
+        each_far_trans(s, lambda c: c.wait_send())
         return carry
 
     lax.fori_loop(0, STEPS, drain, 0)
@@ -446,8 +514,10 @@
         out_specs=(vmem, vmem),
         scratch_shapes=[
             pltpu.VMEM((NS, SLOTS, B, B), BF16),
-            pltpu.VMEM((STEPS, SLOTS, B, B), BF16),
-            pltpu.VMEM((STEPS, SLOTS, B, B), BF16),
+            pltpu.VMEM((STEPS, 2, SLOTS, B, B), BF16),
+            pltpu.VMEM((3, SLOTS, B, B), BF16),
+            pltpu.VMEM((3, 3 * B, B), BF16),
+            pltpu.VMEM((3, B, B), BF16),
             pltpu.VMEM((WM, B, B), BF16),
             pltpu.VMEM((WM, B, B), BF16),
             pltpu.VMEM((PAIRS, 2 * B, B), BF16),
@@ -468,6 +538,10 @@
             dma((NS, SLOTS)),
             dma((STEPS, 2, SLOTS)),
             dma((STEPS, 2, SLOTS)),
+            dma((3, SLOTS)),
+            dma((3, SLOTS)),
+            dma((3,)),
+            dma((3, 2)),
             dma((NS,)),
             dma((NS,)),
             dma((NS,)),

time: 72.3 us -> 70.7 us (0.978)
  Pallas kernels: 68.7 us -> 67.3 us
    pallas_call x1, Pallas kernels: 68.7 us -> 67.3 us  [per_device(): pl.pallas_call(kernel, out_shape=(jax.ShapeDtypeStruct((B, B), F32), jax....]
where the time goes in v3:
time: 70.7 us; the launch traced here: 70.2 us
  Pallas kernels  67.3 us (95%)
  local copies, waits for them, and re-layouts  1.53 us (2%)
  between operations  1.29 us (2%)
    pallas_call x1, Pallas kernels, per_device(): pl.pallas_call(kernel, out_shape=(jax.ShapeDtypeStruct((B, B), F32), jax....  67.3 us
    unnamed x2, local copies, waits for them, and re-layouts  1.53 us

profile of v3, /device:TPU:24, one launch (start us, length us, event | category | flops | bytes accessed | tf_op | source)
XLA Modules:
  0.0 70.2 jit_solution(12007236702281845711)
XLA Ops:
  1.3 67.3 %shard_map.77 = (f32[128,128]{1,0:T(8,128)S(1)}, bf16[26,128,128]{2,1,0:T(8,128)(2,1)S(1)}) custom-call(bf16[26,128,128]{2,1,0:T(8,128)(2,1)} %bitcast.11, bf16[384,128]{1,0:T(8,128)(2,1)} %bitcast.13, f32[26,1,26]{2,1,0:T(1,128)} %bitcast.15, bf16[26,128,128]{2,1,0:T(8,128)(2,1)} %bitcast.12, f32[128,128]{1,0:T(8,128)} %bitcast.14, s32[1]{0:T(128)S(6)} %copy.11.rank), custom_call_target="tpu_custom_call" | custom-call | tf_op jit(solution)/shard_map/pallas_call | solution.py:507
  68.6 0.6 copy.12
  69.3 0.9 %copy.13 = bf16[1,26,1,128,128]{4,3,2,1,0:T(8,128)(2,1)} copy(bf16[1,26,1,128,128]{4,3,2,1,0:T(8,128)(2,1)S(1)} %bitcast.9) | data formatting | bytes 1703936

commit v4 on v3

--- a/solution.py
+++ b/solution.py
@@ -11,6 +11,7 @@
 NS = 8
 NQ = 32
 NX = 4
+NEAR = (1, NQ - 1, 2, NQ - 2)
 SLOTS = 4
 STEPS = NS - 1
 PAIRS = WM // 2
@@ -39,7 +40,7 @@
     start, outbox, inbox, psend, pall,
     load_sem, in_sem, recv_sem, deliver_sem,
     hrecv, hsend, h2recv, h2send, ftrecv, ftsend, trecv, tsend, fsend, mrecv, msend,
-    xrecv, xsem, precv, psem,
+    xrecv, xsem, precv, psem, known,
 ):
     g = lax.axis_index("sec")
     q = lax.axis_index("blk")
@@ -55,6 +56,21 @@
     beyond = jnp.where(x_at == 0, left, right)
     two_off = lax.rem(jnp.where(x_at == 2, q + 2, q + (NQ - 2)), NQ)
 
+    barrier = pltpu.get_barrier_semaphore()
+
+    def greet_sec(i, carry):
+        pl.semaphore_signal(barrier, inc=1, device_id=(lax.rem(g + i, NS), q), device_id_type=MESH)
+        return carry
+
+    lax.fori_loop(1, NS, greet_sec, 0)
+    for i in NEAR:
+        pl.semaphore_signal(barrier, inc=1, device_id=(g, lax.rem(q + i, NQ)), device_id_type=MESH)
+
+    @pl.when(jnp.logical_and(far, core == 0))
+    def _():
+        pl.semaphore_signal(barrier, inc=1, device_id=(g + 1, beyond), device_id_type=MESH)
+
+
     loads = [
         pltpu.make_async_copy(trans_hbm, tall.at[g], in_sem.at[0]),
         pltpu.make_async_copy(mix_hbm, mix_in, in_sem.at[1]),
@@ -76,24 +92,6 @@
         each_slot(j, lambda j=j: load(j).start())
     for c in loads[1:]:
         c.start()
-
-    barrier = pltpu.get_barrier_semaphore()
-
-    def greet_sec(i, carry):
-        pl.semaphore_signal(barrier, inc=1, device_id=(lax.rem(g + i, NS), q), device_id_type=MESH)
-        return carry
-
-    def greet_blk(i, carry):
-        pl.semaphore_signal(barrier, inc=1, device_id=(g, lax.rem(q + i, NQ)), device_id_type=MESH)
-        return carry
-
-    lax.fori_loop(1, NS, greet_sec, 0)
-    lax.fori_loop(1, NQ, greet_blk, 0)
-
-    @pl.when(jnp.logical_and(far, core == 0))
-    def _():
-        pl.semaphore_signal(barrier, inc=1, device_id=(g + 1, beyond), device_id_type=MESH)
-
 
     @pl.when(g == 0)
     def _():
@@ -122,7 +120,7 @@
     for j in range(SLOTS):
         each_slot(j, lambda j=j: load(j).wait())
 
-    pl.semaphore_wait(barrier, NS - 1 + NQ - 1 + jnp.where(jnp.logical_and(far, core == 1), 1, 0))
+    pl.semaphore_wait(barrier, NS - 1 + len(NEAR) + jnp.where(jnp.logical_and(far, core == 1), 1, 0))
 
     def crossed(s):
         return jnp.logical_or(s == 0, lax.rem(s, 2) == 1)
@@ -252,7 +250,24 @@
 
     pass_on(1)
 
+    def tell(i):
+        far_off = 2 << i
+        for other in (q + far_off, q + (NQ - far_off)):
+            pl.semaphore_signal(known.at[i], inc=1, device_id=(g, lax.rem(other, NQ)), device_id_type=MESH)
+
+    def heard(i):
+        pl.semaphore_wait(known.at[i], 2)
+
+    tell(0)
+
     def step(s, carry):
+        for i in range(3):
+            @pl.when(s == i + 1)
+            def _():
+                heard(i)
+                if i < 2:
+                    tell(i + 1)
+
         @pl.when(jnp.logical_and(g != s, jnp.logical_not(forwards(s))))
         def _():
             wait_trans(s)
@@ -551,6 +566,7 @@
             dma((len(SENDS),)),
             dma,
             dma,
+            pltpu.SemaphoreType.REGULAR((3,)),
         ],
         compiler_params=pltpu.CompilerParams(
             collective_id=0, has_side_effects=True, vmem_limit_bytes=40 * 1024 * 1024

time: 70.7 us -> 69.7 us (0.986)
  the two profiles are of different devices: /device:TPU:24 before, /device:TPU:2 now
where the time goes in v4:
time: 69.7 us; the launch traced here: 69.6 us
  Pallas kernels  66.8 us (96%)
  local copies, waits for them, and re-layouts  1.53 us (2%)
  between operations  1.29 us (2%)
    pallas_call x1, Pallas kernels, per_device(): pl.pallas_call(kernel, out_shape=(jax.ShapeDtypeStruct((B, B), F32), jax....  66.8 us
    unnamed x2, local copies, waits for them, and re-layouts  1.53 us

profile of v4, /device:TPU:2, one launch (start us, length us, event | category | flops | bytes accessed | tf_op | source)
XLA Modules:
  0.0 69.6 jit_solution(3261503205168117250)
XLA Ops:
  1.3 66.8 %shard_map.77 = (f32[128,128]{1,0:T(8,128)S(1)}, bf16[26,128,128]{2,1,0:T(8,128)(2,1)S(1)}) custom-call(bf16[26,128,128]{2,1,0:T(8,128)(2,1)} %bitcast.11, bf16[384,128]{1,0:T(8,128)(2,1)} %bitcast.13, f32[26,1,26]{2,1,0:T(1,128)} %bitcast.15, bf16[26,128,128]{2,1,0:T(8,128)(2,1)} %bitcast.12, f32[128,128]{1,0:T(8,128)} %bitcast.14, s32[1]{0:T(128)S(6)} %copy.11.rank), custom_call_target="tpu_custom_call" | custom-call | tf_op jit(solution)/shard_map/pallas_call | solution.py:522
  68.0 0.6 copy.12
  68.7 0.9 %copy.13 = bf16[1,26,1,128,128]{4,3,2,1,0:T(8,128)(2,1)} copy(bf16[1,26,1,128,128]{4,3,2,1,0:T(8,128)(2,1)S(1)} %bitcast.9) | data formatting | bytes 1703936

commit v5 on v4

--- a/solution.py
+++ b/solution.py
@@ -272,7 +272,6 @@
         def _():
             wait_trans(s)
 
-        pass_on(s + 2)
         redo = jnp.logical_and(far, lax.rem(s, 2) == 1)
 
         for d in range(3):
@@ -305,6 +304,11 @@
                     deliver_local(s + 1, j).start()
 
             each_slot(j, body)
+
+        @pl.when(s == 0)
+        def _():
+            for i in range(2, STEPS):
+                pass_on(i)
 
         @pl.when(redo)
         def _():

time: 69.7 us -> 69.1 us (level)
  the two profiles are of different devices: /device:TPU:2 before, /device:TPU:24 now
where the time goes in v5:
time: 69.1 us; the launch traced here: 68.7 us
  Pallas kernels  65.9 us (95%)
  local copies, waits for them, and re-layouts  1.53 us (2%)
  between operations  1.29 us (2%)
    pallas_call x1, Pallas kernels, per_device(): pl.pallas_call(kernel, out_shape=(jax.ShapeDtypeStruct((B, B), F32), jax....  65.9 us
    unnamed x2, local copies, waits for them, and re-layouts  1.53 us

profile of v5, /device:TPU:24, one launch (start us, length us, event | category | flops | bytes accessed | tf_op | source)
XLA Modules:
  0.0 68.7 jit_solution(12619173027545763893)
XLA Ops:
  1.3 65.9 %shard_map.77 = (f32[128,128]{1,0:T(8,128)S(1)}, bf16[26,128,128]{2,1,0:T(8,128)(2,1)S(1)}) custom-call(bf16[26,128,128]{2,1,0:T(8,128)(2,1)} %bitcast.11, bf16[384,128]{1,0:T(8,128)(2,1)} %bitcast.13, f32[26,1,26]{2,1,0:T(1,128)} %bitcast.15, bf16[26,128,128]{2,1,0:T(8,128)(2,1)} %bitcast.12, f32[128,128]{1,0:T(8,128)} %bitcast.14, s32[1]{0:T(128)S(6)} %copy.11.rank), custom_call_target="tpu_custom_call" | custom-call | tf_op jit(solution)/shard_map/pallas_call | solution.py:526
  67.2 0.6 copy.12
  67.8 0.9 %copy.13 = bf16[1,26,1,128,128]{4,3,2,1,0:T(8,128)(2,1)} copy(bf16[1,26,1,128,128]{4,3,2,1,0:T(8,128)(2,1)S(1)} %bitcast.9) | data formatting | bytes 1703936

commit v6 on v5

--- a/solution.py
+++ b/solution.py
@@ -11,7 +11,7 @@
 NS = 8
 NQ = 32
 NX = 4
-NEAR = (1, NQ - 1, 2, NQ - 2)
+NEAR = (1, -1, 2, -2)
 SLOTS = 4
 STEPS = NS - 1
 PAIRS = WM // 2
@@ -51,7 +51,15 @@
     first = 3 * g + jnp.where(g >= 1, 1, 0) + jnp.where(g >= 3, 1, 0)
     four = jnp.logical_or(g == 0, g == 2)
     x_at = lax.rem(q, NX)
-    far = jnp.logical_or(x_at == 0, x_at == NX - 1)
+    low_end, high_end = q == 0, q == NQ - 1
+    at_low = jnp.logical_and(x_at == 0, jnp.logical_not(low_end))
+    at_high = jnp.logical_and(x_at == NX - 1, jnp.logical_not(high_end))
+    far = jnp.logical_or(at_low, at_high)
+    gives = jnp.logical_or(jnp.logical_and(x_at == 1, q > NX), jnp.logical_and(x_at == 2, q < NQ - NX))
+
+    def exists(other):
+        return jnp.logical_and(other >= 0, other < NQ)
+
     side = jnp.where(x_at == 0, 0, 1)
     beyond = jnp.where(x_at == 0, left, right)
     two_off = lax.rem(jnp.where(x_at == 2, q + 2, q + (NQ - 2)), NQ)
@@ -63,8 +71,13 @@
         return carry
 
     lax.fori_loop(1, NS, greet_sec, 0)
+    greeted = NS - 1 + jnp.where(jnp.logical_and(far, core == 1), 1, 0)
     for i in NEAR:
-        pl.semaphore_signal(barrier, inc=1, device_id=(g, lax.rem(q + i, NQ)), device_id_type=MESH)
+        @pl.when(exists(q + i))
+        def _():
+            pl.semaphore_signal(barrier, inc=1, device_id=(g, q + i), device_id_type=MESH)
+
+        greeted += jnp.where(exists(q + i), 1, 0)
 
     @pl.when(jnp.logical_and(far, core == 0))
     def _():
@@ -102,6 +115,15 @@
         lax.fori_loop(0, WM, body, 0)
 
     own_mix[...] = jnp.zeros_like(own_mix)
+    for end, at in ((low_end, 0), (high_end, 1)):
+        @pl.when(end)
+        def _():
+            def clear(s, carry):
+                halo[s, at] = jnp.zeros((SLOTS, B, B), BF16)
+                return carry
+
+            lax.fori_loop(0, STEPS, clear, 0)
+
     loads[1].wait()
     own_mix[:WM, :WM] = mix_in[...].reshape(WM, WM)
     mixall[g] = own_mix[...]
@@ -120,7 +142,7 @@
     for j in range(SLOTS):
         each_slot(j, lambda j=j: load(j).wait())
 
-    pl.semaphore_wait(barrier, NS - 1 + len(NEAR) + jnp.where(jnp.logical_and(far, core == 1), 1, 0))
+    pl.semaphore_wait(barrier, greeted)
 
     def crossed(s):
         return jnp.logical_or(s == 0, lax.rem(s, 2) == 1)
@@ -132,16 +154,17 @@
             device_id=(g, right if to else left), device_id_type=MESH,
         )
 
-    def inside(to):
-        return x_at != (NX - 1 if to else 0)
+    def meets(to, s):
+        end, at = (high_end, at_high) if to else (low_end, at_low)
+        return jnp.logical_and(jnp.logical_not(end), jnp.logical_or(jnp.logical_not(at), crossed(s)))
 
     def each_halo(s, j, act):
         for to in range(2):
-            pl.when(jnp.logical_or(inside(to), crossed(s)))(lambda to=to: act(halo_copy(s, j, to)))
+            pl.when(meets(to, s))(lambda to=to: act(halo_copy(s, j, to)))
 
     def wait_halo(s, j):
         for at in range(2):
-            @pl.when(jnp.logical_or(inside(at), crossed(s)))
+            @pl.when(meets(at, s))
             def _():
                 halo_copy(s, j, 1 - at).wait_recv()
 
@@ -153,7 +176,7 @@
         )
 
     def each_halo2(s, j, act):
-        pl.when(jnp.logical_and(jnp.logical_not(far), lax.rem(s, 2) == 1))(lambda: act(halo2_copy(s, j)))
+        pl.when(jnp.logical_and(gives, lax.rem(s, 2) == 1))(lambda: act(halo2_copy(s, j)))
 
     def start_halo(s, j):
         each_halo(s, j, lambda c: c.start())
@@ -215,7 +238,7 @@
     def send(m):
         for i in range(len(SENDS)):
             if SENDS[i][0] == m:
-                box_copy(i).start()
+                pl.when(exists(q + SENDS[i][1]))(lambda i=i: box_copy(i).start())
 
     send(0)
 
@@ -251,21 +274,23 @@
     pass_on(1)
 
     def tell(i):
-        far_off = 2 << i
-        for other in (q + far_off, q + (NQ - far_off)):
-            pl.semaphore_signal(known.at[i], inc=1, device_id=(g, lax.rem(other, NQ)), device_id_type=MESH)
+        for other in (q + (2 << i), q - (2 << i)):
+            @pl.when(exists(other))
+            def _():
+                pl.semaphore_signal(known.at[i], inc=1, device_id=(g, other), device_id_type=MESH)
 
     def heard(i):
-        pl.semaphore_wait(known.at[i], 2)
+        count = sum(jnp.where(exists(other), 1, 0) for other in (q + (2 << i), q - (2 << i)))
+        pl.semaphore_wait(known.at[i], count)
 
     tell(0)
 
     def step(s, carry):
-        for i in range(3):
+        for i in range(4):
             @pl.when(s == i + 1)
             def _():
                 heard(i)
-                if i < 2:
+                if i < 3:
                     tell(i + 1)
 
         @pl.when(jnp.logical_and(g != s, jnp.logical_not(forwards(s))))
@@ -402,14 +427,18 @@
 
     def take(m, far):
         i = SENDS.index((m, far))
-        box_copy(i).wait_recv()
-        there = jnp.logical_and(q - far >= 0, q - far < NQ)
+        there = exists(q - far)
+
+        @pl.when(there)
+        def _():
+            box_copy(i).wait_recv()
+
         value = jnp.where(there, inbox[i, :B, :].astype(F32), 0.0)
         return value, inbox[i, B:, :].astype(F32)[:1, :1]
 
     def take_scaled(m, far):
         value, e = take(m, far)
-        return value, 2.0 * e
+        return value, jnp.where(exists(q - far), 2.0 * e, -1000.0)
 
     def size(m, e):
         return log2(total(m * m)) + 2.0 * e
@@ -446,8 +475,8 @@
     mp_r, lp_r = take_scaled(2, -1)
     m2_l, l2_l = add([(mp_l, lp_l), (half_l * m1, l1), (half_l * m1_ll, l1_ll)])
     m2_r, l2_r = add([(mp_r, lp_r), (half_r * m1, l1), (half_r * m1_rr, l1_rr)])
-    m2_l = jnp.where(q > 0, m2_l, 0.0)
-    m2_r = jnp.where(q < NQ - 1, m2_r, 0.0)
+    m2_l, l2_l = jnp.where(low_end, 0.0, m2_l), jnp.where(low_end, -1000.0, l2_l)
+    m2_r, l2_r = jnp.where(high_end, 0.0, m2_r), jnp.where(high_end, -1000.0, l2_r)
     m3, l3 = norm(*add([(r, lr), (half * m2_l, l2_l), (half * m2_r, l2_r)]))
     x3 = m3.astype(BF16)
     post(3, x3, l3)
@@ -508,7 +537,7 @@
             mix_copy(i).wait_send()
 
     for i in range(len(SENDS)):
-        box_copy(i).wait_send()
+        pl.when(exists(q + SENDS[i][1]))(lambda i=i: box_copy(i).wait_send())
     others = pall.at[pl.ds(0, NQ - 1)]
     pltpu.make_async_copy(others, others, psem).wait()
     pltpu.make_async_copy(others, others, precv).wait()
@@ -570,7 +599,7 @@
             dma((len(SENDS),)),
             dma,
             dma,
-            pltpu.SemaphoreType.REGULAR((3,)),
+            pltpu.SemaphoreType.REGULAR((4,)),
         ],
         compiler_params=pltpu.CompilerParams(
             collective_id=0, has_side_effects=True, vmem_limit_bytes=40 * 1024 * 1024

time: 69.1 us -> 69.1 us (level)
  no operation moved by 1% of the time
where the time goes in v6:
time: 69.1 us; the launch traced here: 68.8 us
  Pallas kernels  66 us (96%)
  local copies, waits for them, and re-layouts  1.53 us (2%)
  between operations  1.29 us (2%)
    pallas_call x1, Pallas kernels, per_device(): pl.pallas_call(kernel, out_shape=(jax.ShapeDtypeStruct((B, B), F32), jax....  66 us
    unnamed x2, local copies, waits for them, and re-layouts  1.53 us

profile of v6, /device:TPU:24, one launch (start us, length us, event | category | flops | bytes accessed | tf_op | source)
XLA Modules:
  0.0 68.8 jit_solution(10549320736421930775)
XLA Ops:
  1.3 66.0 %shard_map.77 = (f32[128,128]{1,0:T(8,128)S(1)}, bf16[26,128,128]{2,1,0:T(8,128)(2,1)S(1)}) custom-call(bf16[26,128,128]{2,1,0:T(8,128)(2,1)} %bitcast.11, bf16[384,128]{1,0:T(8,128)(2,1)} %bitcast.13, f32[26,1,26]{2,1,0:T(1,128)} %bitcast.15, bf16[26,128,128]{2,1,0:T(8,128)(2,1)} %bitcast.12, f32[128,128]{1,0:T(8,128)} %bitcast.14, s32[1]{0:T(128)S(6)} %copy.11.rank), custom_call_target="tpu_custom_call" | custom-call | tf_op jit(solution)/shard_map/pallas_call | solution.py:555
  67.3 0.6 copy.12
  67.9 0.9 %copy.13 = bf16[1,26,1,128,128]{4,3,2,1,0:T(8,128)(2,1)} copy(bf16[1,26,1,128,128]{4,3,2,1,0:T(8,128)(2,1)S(1)} %bitcast.9) | data formatting | bytes 1703936

commit v7 on v6

--- a/solution.py
+++ b/solution.py
@@ -19,10 +19,10 @@
 KR = WM * ROWS
 FIRSTS = (0, 4, 7, 11, 14, 17, 20, 23)
 ORDER = [f + j for j in range(3) for f in FIRSTS] + [3, 10]
-GROUPS = (range(0, 4), range(4, 8), range(8, 13))
+GROUPS = (range(0, 8), range(8, 13))
 AUX = 16
 MSG = B + AUX
-SENDS = ((0, 1), (0, -1), (1, 1), (1, -1), (1, 2), (1, -2), (2, 1), (2, -1), (3, 1), (3, -1))
+SENDS = ((0, 1), (0, -1), (1, 2), (1, -2), (1, 1), (1, -1), (2, 1), (2, -1), (3, 1), (3, -1))
 LOG_EPS = -19.931568569324174
 LOG_N = 19.0
 MESH = pl.DeviceIdType.MESH
@@ -223,11 +223,6 @@
         each_slot(j, lambda j=j: start_halo(0, j))
     each_trans(lambda c: c.start())
 
-    @pl.when(g < STEPS)
-    def _():
-        for i in range(1, NS):
-            mix_copy(i).start()
-
     def box_copy(i):
         m, far = SENDS[i]
         return pltpu.make_async_remote_copy(
@@ -284,6 +279,16 @@
         pl.semaphore_wait(known.at[i], count)
 
     tell(0)
+
+    def multiply(s):
+        @pl.when(g != s)
+        def _():
+            pltpu.make_async_copy(mixall.at[s], mixall.at[s], mrecv.at[s]).wait()
+
+        @pl.when(s < g)
+        def _():
+            amat[...] = jnp.dot(mixall[s][:, :32], amat[...], precision=lax.Precision.HIGHEST, preferred_element_type=F32)
+
 
     def step(s, carry):
         for i in range(4):
@@ -334,6 +339,11 @@
         def _():
             for i in range(2, STEPS):
                 pass_on(i)
+
+            @pl.when(g < STEPS)
+            def _():
+                for i in range(1, NS):
+                    mix_copy(i).start()
 
         @pl.when(redo)
         def _():
@@ -350,17 +360,12 @@
 
                 each_slot(j, again)
 
-        @pl.when(g != s)
-        def _():
-            pltpu.make_async_copy(mixall.at[s], mixall.at[s], mrecv.at[s]).wait()
-
-        @pl.when(s < g)
-        def _():
-            amat[...] = jnp.dot(mixall[s][:, :32], amat[...], precision=lax.Precision.HIGHEST, preferred_element_type=F32)
-
+        pl.when(s >= 3)(lambda: multiply(s - 3))
         return carry
 
     lax.fori_loop(0, STEPS, step, 0)
+    for s in range(STEPS - 3, STEPS):
+        multiply(s)
 
     a = amat[...][:, :32].astype(BF16)
     wide = lax.broadcasted_iota(jnp.int32, (KR, 32), 0) // ROWS

time: 69.1 us -> 68.6 us (level)
  no operation moved by 1% of the time
where the time goes in v7:
time: 68.6 us; the launch traced here: 68.5 us
  Pallas kernels  65.6 us (96%)
  local copies, waits for them, and re-layouts  1.53 us (2%)
  between operations  1.29 us (2%)
    pallas_call x1, Pallas kernels, per_device(): pl.pallas_call(kernel, out_shape=(jax.ShapeDtypeStruct((B, B), F32), jax....  65.6 us
    unnamed x2, local copies, waits for them, and re-layouts  1.53 us

profile of v7, /device:TPU:24, one launch (start us, length us, event | category | flops | bytes accessed | tf_op | source)
XLA Modules:
  0.0 68.5 jit_solution(7155708481999703792)
XLA Ops:
  1.3 65.6 %shard_map.77 = (f32[128,128]{1,0:T(8,128)S(1)}, bf16[26,128,128]{2,1,0:T(8,128)(2,1)S(1)}) custom-call(bf16[26,128,128]{2,1,0:T(8,128)(2,1)} %bitcast.11, bf16[384,128]{1,0:T(8,128)(2,1)} %bitcast.13, f32[26,1,26]{2,1,0:T(1,128)} %bitcast.15, bf16[26,128,128]{2,1,0:T(8,128)(2,1)} %bitcast.12, f32[128,128]{1,0:T(8,128)} %bitcast.14, s32[1]{0:T(128)S(6)} %copy.11.rank), custom_call_target="tpu_custom_call" | custom-call | tf_op jit(solution)/shard_map/pallas_call | solution.py:560
  66.9 0.6 copy.12
  67.6 0.9 %copy.13 = bf16[1,26,1,128,128]{4,3,2,1,0:T(8,128)(2,1)} copy(bf16[1,26,1,128,128]{4,3,2,1,0:T(8,128)(2,1)S(1)} %bitcast.9) | data formatting | bytes 1703936

commit v8 on v7

--- a/solution.py
+++ b/solution.py
@@ -19,7 +19,7 @@
 KR = WM * ROWS
 FIRSTS = (0, 4, 7, 11, 14, 17, 20, 23)
 ORDER = [f + j for j in range(3) for f in FIRSTS] + [3, 10]
-GROUPS = (range(0, 8), range(8, 13))
+GROUPS = (range(0, 13),)
 AUX = 16
 MSG = B + AUX
 SENDS = ((0, 1), (0, -1), (1, 2), (1, -2), (1, 1), (1, -1), (2, 1), (2, -1), (3, 1), (3, -1))

time: 68.6 us -> 68.9 us (level)
  no operation moved by 1% of the time
where the time goes in v8:
time: 68.9 us; the launch traced here: 68.8 us
  Pallas kernels  66 us (96%)
  local copies, waits for them, and re-layouts  1.53 us (2%)
  between operations  1.29 us (2%)
    pallas_call x1, Pallas kernels, per_device(): pl.pallas_call(kernel, out_shape=(jax.ShapeDtypeStruct((B, B), F32), jax....  66 us
    unnamed x2, local copies, waits for them, and re-layouts  1.53 us

profile of v8, /device:TPU:24, one launch (start us, length us, event | category | flops | bytes accessed | tf_op | source)
XLA Modules:
  0.0 68.8 jit_solution(8362533867475866515)
XLA Ops:
  1.3 66.0 %shard_map.77 = (f32[128,128]{1,0:T(8,128)S(1)}, bf16[26,128,128]{2,1,0:T(8,128)(2,1)S(1)}) custom-call(bf16[26,128,128]{2,1,0:T(8,128)(2,1)} %bitcast.11, bf16[384,128]{1,0:T(8,128)(2,1)} %bitcast.13, f32[26,1,26]{2,1,0:T(1,128)} %bitcast.15, bf16[26,128,128]{2,1,0:T(8,128)(2,1)} %bitcast.12, f32[128,128]{1,0:T(8,128)} %bitcast.14, s32[1]{0:T(128)S(6)} %copy.11.rank), custom_call_target="tpu_custom_call" | custom-call | tf_op jit(solution)/shard_map/pallas_call | solution.py:560
  67.3 0.6 copy.12
  67.9 0.9 %copy.13 = bf16[1,26,1,128,128]{4,3,2,1,0:T(8,128)(2,1)} copy(bf16[1,26,1,128,128]{4,3,2,1,0:T(8,128)(2,1)S(1)} %bitcast.9) | data formatting | bytes 1703936
